TPU v7x, 32 devices: a whole 2x2x4 slice. The times are simulated.
32 devices in a mesh: row: 4 (over y, core), col: 8 (over z, x).
Axes of the slice: x: 2, y: 2, z: 4, core: 2. Of those that a mesh axis runs over, the one named last changes fastest.
Arguments:
- pair_features: bfloat16 [64, 512, 512], P(None, 'col', 'row'), may hold values from -6 to 6
- first_block_kernel: bfloat16 [3, 3, 64, 64], replicated, may hold values from -0.25 to 0.25
- first_block_bias: float32 [64], replicated, may hold values from -3 to 3
- second_block_kernel: bfloat16 [3, 3, 64, 64], replicated, may hold values from -0.25 to 0.25
- second_block_bias: float32 [64], replicated, may hold values from -3 to 3
- head_weight: bfloat16 [37, 64], replicated, may hold values from -32 to 32
- head_bias: float32 [37], replicated, may hold values from -4 to 4
- target: int32 [512, 512], P('col', 'row'), may hold values from 0 to 36
Outputs:
- feat_grad: float32 [64, 512, 512], P(None, 'col', 'row')
All inputs are finite; a program needn't handle non-finite values.
Results may differ from a plain program's by a relative error of at most 0.0055.
The roundings to bfloat16 on the way count: a program that leaves them out, or rounds other values in their place, can miss the bound.
Values may be sent and summed in bfloat16 or wider, within the bound.
No kernel may reach another device: no remote copies, remote signals or barrier semaphores. Data moves between devices by JAX's collectives and lax.ppermute only.
A program may use at most 64 MiB of HBM per device.

v0:
```python
import functools

import jax
import jax.numpy as jnp
from jax import lax
from jax.experimental import pallas as pl
from jax.experimental.pallas import tpu as pltpu
from jax.sharding import PartitionSpec as P

DILATION_FIRST = 4
DILATION_SECOND = 8
MARGIN = DILATION_FIRST + DILATION_SECOND
SLOT = 16
F32 = jnp.float32
BF16 = jnp.bfloat16
VMEM = pl.BlockSpec(memory_space=pltpu.VMEM)
SMEM = pl.BlockSpec(memory_space=pltpu.SMEM)


def params(megabytes):
    return pltpu.CompilerParams(vmem_limit_bytes=megabytes << 20)


def lanes_of(shape):
    return lax.broadcasted_iota(jnp.int32, shape, len(shape) - 1)


def pack_edges(rows, first_ref, second_ref, block):
    count = len(rows)
    width = rows[0].shape[-1]
    slot = lanes_of(rows[0].shape) // SLOT
    first = second = None
    for i, row in enumerate(rows):
        turned = pltpu.roll(row, SLOT * i, 1) if i else row
        first = turned if first is None else jnp.where(slot == i, turned, first)
        second = turned if second is None else jnp.where(slot == (i - 1) % count, turned, second)
    first_ref[block] = first.astype(BF16)
    second_ref[block] = second.astype(BF16)


def ring_row(main, right, left, i):
    width = main.shape[-1]
    lane = lanes_of(main.shape)
    both = jnp.where(lane // SLOT == i, right.astype(F32), left.astype(F32))
    if i:
        both = pltpu.roll(both, width - SLOT * i, 1)
    edge = jnp.where((lane < MARGIN) | (lane >= width - MARGIN), both, 0.0)
    return jnp.concatenate([main, edge.astype(BF16)], axis=1)


def build_ring(top_ref, main_ref, right_ref, left_ref, bottom_ref, ring_ref):
    size = main_ref.shape[0]
    per = main_ref.shape[-1] // SLOT
    shift = (-MARGIN) % per
    near = (MARGIN + per - 1) // per
    for e in range(MARGIN):
        block, slot = divmod(e + shift, per)
        ring_ref[e] = ring_row(
            top_ref[e], top_ref[MARGIN + block], top_ref[MARGIN + near + block], slot
        )
        block, slot = divmod(e, per)
        ring_ref[MARGIN + size + e] = ring_row(
            bottom_ref[e], bottom_ref[MARGIN + block], bottom_ref[MARGIN + near + block], slot
        )

    @pl.loop(0, size // per)
    def _(block):
        right = right_ref[block]
        left = left_ref[block]
        for slot in range(per):
            row = block * per + slot
            ring_ref[MARGIN + row] = ring_row(main_ref[row], right, left, slot)


def taps(row, spacing, width):
    wide = row.astype(F32)
    full = row.shape[-1]
    back = pltpu.roll(wide, spacing, 1)[:, :width]
    ahead = pltpu.roll(wide, full - spacing, 1)[:, :width]
    return jnp.concatenate([back.astype(BF16), row[:, :width], ahead.astype(BF16)], axis=0)


def wide_conv(source_ref, weights, spacing, sums_ref, finish, unroll):
    rows, channels, full = source_ref.shape

    def step(e, last):
        z = jnp.dot(weights, taps(source_ref[e], spacing, full), preferred_element_type=F32)
        if last:
            finish(e - 2 * spacing, sums_ref[e] + z[2 * channels :])
        sums_ref[e + spacing] += z[channels : 2 * channels]
        sums_ref[e + 2 * spacing] = z[:channels]

    run(rows, spacing, step, unroll)


def run(rows, spacing, step, unroll):
    @pl.loop(0, 2 * spacing, step=unroll)
    def _(e):
        for k in range(unroll):
            step(e + k, False)

    @pl.loop(2 * spacing, rows, step=unroll)
    def _(e):
        for k in range(unroll):
            step(e + k, True)


def narrow_conv(source_ref, weights, spacing, sums_ref, finish, unroll):
    rows, channels, full = source_ref.shape
    width = full // 2

    def step(half, last):
        e = 2 * half
        both = jnp.concatenate(
            [taps(source_ref[e + k], spacing, width) for k in range(2)], axis=1
        )
        z = jnp.dot(weights, both, preferred_element_type=F32)
        if last:
            finish(half - spacing, sums_ref[half] + z[2 * channels :])
        sums_ref[half + spacing // 2] += z[channels : 2 * channels]
        sums_ref[half + spacing] = z[:channels]

    run(rows // 2, spacing // 2, step, unroll)


def prepare_kernel(x_ref, xt_ref, first_ref, second_ref):
    channels, size, width = x_ref.shape
    per = width // SLOT

    @pl.loop(0, size // per)
    def _(block):
        chunk = x_ref[:, pl.ds(block * per, per), :].astype(F32)
        turned = jnp.swapaxes(chunk, 0, 1)
        xt_ref[pl.ds(block * per, per)] = turned.astype(BF16)
        pack_edges([turned[i] for i in range(per)], first_ref, second_ref, block)


def forward_kernel(
    place_ref, top_ref, main_ref, right_ref, left_ref, bottom_ref, target_ref,
    w1_ref, b1_ref, w2_ref, b2_ref,
    hidden_ref, slope_one_ref, slope_two_ref, send_ref,
    ring_ref, hidden_ring_ref, sums_ref,
):
    size, channels, width = main_ref.shape
    d1, d2 = DILATION_FIRST, DILATION_SECOND
    build_ring(top_ref, main_ref, right_ref, left_ref, bottom_ref, ring_ref)
    col, row, cols, rows = (place_ref[k] for k in range(4))
    lane = lanes_of((1, 2 * width))
    q = jnp.where(lane < width + width // 2, lane, lane - 2 * width) + row * width
    lane_ok = jnp.where((q >= 0) & (q < rows * width), 1.0, 0.0)
    w1 = w1_ref[...]
    w2 = w2_ref[...]
    b1 = b1_ref[...]
    b2 = b2_ref[...]

    def finish_one(o, total):
        pre = total + ring_ref[o + d1].astype(F32) + b1
        decay = jnp.exp(jnp.minimum(pre, 0.0))
        up = pre > 0
        p = o - d2 + col * size
        ok = lane_ok * jnp.where((p >= 0) & (p < cols * size), 1.0, 0.0)
        hidden_ring_ref[o] = (jnp.where(up, pre, decay - 1.0) * ok).astype(BF16)
        slope_one_ref[o] = jnp.where(up, 1.0, decay) * ok

    wide_conv(ring_ref, w1, d1, sums_ref, finish_one, 4)

    group = width // size
    mine = lax.rem(col, group)
    low = lanes_of((channels // 2, width)) < size

    def send(p, hidden):
        lo, hi = hidden[: channels // 2], hidden[channels // 2 :]
        send_ref[mine, p] = jnp.where(low, lo, pltpu.roll(hi, size, 1)).astype(BF16)
        send_ref[1 - mine, p] = jnp.where(low, pltpu.roll(lo, size, 1), hi).astype(BF16)

    def finish_two(half, total):
        for k in range(2):
            p = 2 * half + k
            pre = (
                total[:, k * width : (k + 1) * width]
                + hidden_ring_ref[p + d2, :, :width].astype(F32)
                + b2
            )
            decay = jnp.exp(jnp.minimum(pre, 0.0))
            up = pre > 0
            hidden = jnp.where(up, pre, decay - 1.0)
            hidden_ref[p] = hidden.astype(BF16)
            slope_two_ref[p] = jnp.where(up, 1.0, decay)
            send(p, hidden)

    narrow_conv(hidden_ring_ref, w2, d2, sums_ref, finish_two, 4)
    label = target_ref[...].astype(F32)
    send(size, label)


def head_kernel(
    place_ref, received_a_ref, received_b_ref, hidden_ref, slope_two_ref, target_ref,
    weight_ref, weight_t_ref, bias_ref,
    delta_ref, first_ref, second_ref,
    wide_ref, turned_ref, target_t_ref,
):
    size, channels, width = hidden_ref.shape
    half = channels // 2
    group = width // size
    mine = lax.rem(place_ref[0], group)

    @pl.loop(0, size, step=8)
    def _(p):
        for k in range(8):
            wide_ref[pl.ds((mine * size + p + k) * half, half), :] = received_a_ref[p + k].astype(F32)
            wide_ref[pl.ds(((1 - mine) * size + p + k) * half, half), :] = received_b_ref[p + k].astype(F32)

    @pl.loop(0, half, step=2)
    def _(c):
        for k in range(2):
            page = wide_ref[pl.ds(c + k, width, stride=half), :]
            page = page.T
            turned_ref[pl.ds(c + k, size, stride=channels), :] = page[:size]
            turned_ref[pl.ds(c + k + half, size, stride=channels), :] = page[size:]

    label_a = received_a_ref[size].astype(F32)
    label_b = received_b_ref[size].astype(F32)
    by_place = [
        jnp.where(mine == 0, label_a, label_b),
        jnp.where(mine == 0, label_b, label_a),
    ]
    page = jnp.concatenate(
        [by_place[0], pltpu.roll(by_place[0], size, 1), by_place[1], pltpu.roll(by_place[1], size, 1)],
        axis=0,
    )
    target_t_ref[...] = page.T[:size].astype(jnp.int32)

    bins = weight_ref.shape[0]
    weight = weight_ref[...]
    weight_t = weight_t_ref[...]
    bias = bias_ref[...]
    bin_id = lax.broadcasted_iota(jnp.int32, (bins, 2 * width), 0)
    per = width // SLOT

    def pair(p):
        symmetric = jnp.concatenate(
            [
                (
                    hidden_ref[p + k].astype(F32)
                    + turned_ref[pl.ds((p + k) * channels, channels), :]
                ).astype(BF16)
                for k in range(2)
            ],
            axis=1,
        )
        logits = jnp.dot(weight, symmetric, preferred_element_type=F32) + bias
        top = jnp.max(logits, axis=0, keepdims=True)
        raised = jnp.exp(logits - top)
        probability = raised / jnp.sum(raised, axis=0, keepdims=True)
        labels = [
            jnp.concatenate([ref[pl.ds(p + k, 1), :] for k in range(2)], axis=1)
            for ref in (target_ref, target_t_ref)
        ]
        grads = [
            (probability - jnp.where(bin_id == label, 1.0, 0.0)).astype(BF16).astype(F32)
            for label in labels
        ]
        bins_sum = (grads[0] + grads[1]).astype(BF16)
        grad_two = jnp.dot(weight_t, bins_sum, preferred_element_type=F32)
        return [
            (grad_two[:, k * width : (k + 1) * width] * slope_two_ref[p + k]).astype(BF16)
            for k in range(2)
        ]

    @pl.loop(0, size // per)
    def _(block):
        deltas = []
        for k in range(0, per, 2):
            deltas += pair(block * per + k)
        for k in range(per):
            delta_ref[block * per + k] = deltas[k]
        pack_edges([d.astype(F32) for d in deltas], first_ref, second_ref, block)


def backward_kernel(
    top_ref, main_ref, right_ref, left_ref, bottom_ref, slope_one_ref, w2_ref, w1_ref,
    out_ref,
    ring_ref, delta_ring_ref, sums_ref,
):
    size, channels, width = main_ref.shape
    d1, d2 = DILATION_FIRST, DILATION_SECOND
    build_ring(top_ref, main_ref, right_ref, left_ref, bottom_ref, ring_ref)
    w2 = w2_ref[...]
    w1 = w1_ref[...]

    def finish_one(o, total):
        grad = total + ring_ref[o + d2].astype(F32)
        delta_ring_ref[o] = (grad * slope_one_ref[o + d2 - d1]).astype(BF16)

    wide_conv(ring_ref, w2, d2, sums_ref, finish_one, 4)

    def finish_two(half, total):
        for k in range(2):
            p = 2 * half + k
            out_ref[pl.ds(p, channels, stride=size), :] = (
                total[:, k * width : (k + 1) * width]
                + delta_ring_ref[p + d1, :, :width].astype(F32)
            )

    narrow_conv(delta_ring_ref, w1, d1, sums_ref, finish_two, 2)


def shifted(tensor, axis, step):
    count = lax.axis_size(axis)
    pairs = [(i, i + step) for i in range(count) if 0 <= i + step < count]
    return lax.ppermute(tensor, axis, pairs)


def halos(main, first, second):
    right = shifted(first, "row", -1)
    left = shifted(second, "row", 1)
    near = -(-MARGIN // (main.shape[-1] // SLOT))
    top = shifted(jnp.concatenate([main[-MARGIN:], right[-near:], left[-near:]]), "col", 1)
    bottom = shifted(jnp.concatenate([main[:MARGIN], right[:near], left[:near]]), "col", -1)
    return top, main, right, left, bottom


def mirror_pairs(step):
    col_count, row_count = lax.axis_size("col"), lax.axis_size("row")
    group = col_count // row_count
    return [
        (r * col_count + c, (c // group) * col_count + group * r + (c % group + step) % group)
        for c in range(col_count)
        for r in range(row_count)
    ]


def local(
    pair_features,
    first_block_kernel,
    first_block_bias,
    second_block_kernel,
    second_block_bias,
    head_weight,
    head_bias,
    target,
):
    channels, size, width = pair_features.shape
    d1, d2 = DILATION_FIRST, DILATION_SECOND
    per = width // SLOT
    place = jnp.stack(
        [
            lax.axis_index("col"), lax.axis_index("row"),
            jnp.int32(lax.axis_size("col")), jnp.int32(lax.axis_size("row")),
        ]
    ).astype(jnp.int32)

    def ahead(kernel):
        return kernel.transpose(0, 2, 1, 3).reshape(3 * channels, 3 * channels)

    def back(kernel):
        return kernel[::-1, ::-1].transpose(0, 3, 1, 2).reshape(3 * channels, 3 * channels)

    row_type = jax.ShapeDtypeStruct((size, channels, width), BF16)
    pack_type = jax.ShapeDtypeStruct((size // per, channels, width), BF16)
    prepared = pl.pallas_call(
        prepare_kernel,
        out_shape=(row_type, pack_type, pack_type),
        in_specs=[VMEM],
        out_specs=(VMEM,) * 3,
        compiler_params=params(24),
        name="prepare",
    )(pair_features)
    around = halos(*prepared)

    near_rows = size + 2 * d2
    wide_rows = size + 2 * MARGIN
    hidden, slope_one, slope_two, sent = pl.pallas_call(
        forward_kernel,
        out_shape=(
            row_type,
            jax.ShapeDtypeStruct((near_rows, channels, 2 * width), F32),
            jax.ShapeDtypeStruct((size, channels, width), F32),
            jax.ShapeDtypeStruct((2, size + 1, channels // 2, width), BF16),
        ),
        in_specs=[SMEM] + [VMEM] * 10,
        out_specs=(VMEM,) * 4,
        scratch_shapes=[
            pltpu.VMEM((wide_rows, channels, 2 * width), BF16),
            pltpu.VMEM((near_rows, channels, 2 * width), BF16),
            pltpu.VMEM((wide_rows + 2 * d2, channels, 2 * width), F32),
        ],
        compiler_params=params(48),
        name="forward",
    )(
        place, *around, target,
        ahead(first_block_kernel), first_block_bias[:, None],
        ahead(second_block_kernel), second_block_bias[:, None],
    )
    received = [lax.ppermute(sent[k], ("row", "col"), mirror_pairs(k)) for k in range(2)]

    bins = head_weight.shape[0]
    bins_up = -(-bins // 16) * 16
    weight = jnp.pad(head_weight, ((0, bins_up - bins), (0, 0)))
    bias = jnp.pad(head_bias, (0, bins_up - bins), constant_values=-jnp.inf)[:, None]
    delta = pl.pallas_call(
        head_kernel,
        out_shape=(row_type, pack_type, pack_type),
        in_specs=[SMEM] + [VMEM] * 8,
        out_specs=(VMEM,) * 3,
        scratch_shapes=[
            pltpu.VMEM((2 * size * channels // 2, width), F32),
            pltpu.VMEM((size * channels, width), F32),
            pltpu.VMEM((size, width), jnp.int32),
        ],
        compiler_params=params(32),
        name="head",
    )(place, *received, hidden, slope_two, target, weight, weight.T, bias)
    around = halos(*delta)

    out = pl.pallas_call(
        backward_kernel,
        out_shape=jax.ShapeDtypeStruct((channels * size, width), F32),
        in_specs=[VMEM] * 8,
        out_specs=VMEM,
        scratch_shapes=[
            pltpu.VMEM((wide_rows, channels, 2 * width), BF16),
            pltpu.VMEM((near_rows - 2 * d1, channels, 2 * width), BF16),
            pltpu.VMEM((wide_rows + 2 * d2, channels, 2 * width), F32),
        ],
        compiler_params=params(48),
        name="backward",
    )(*around, slope_one, back(second_block_kernel), back(first_block_kernel))
    return out.reshape(channels, size, width)


def solution(mesh):
    in_specs = (P(None, "col", "row"), P(), P(), P(), P(), P(), P(), P("col", "row"))
    out_specs = P(None, "col", "row")
    return jax.shard_map(local, mesh=mesh, in_specs=in_specs, out_specs=out_specs, check_vma=False)
```

profile of v0, /device:TPU:6, one launch (start us, length us, event | category | flops | bytes accessed | tf_op | source)
XLA Modules:
  0.0 151.4 jit_solution(16994364696598607558)
XLA Ops:
  0.0 1.2 copy-done.1
  1.2 1.3 prepare.1
  2.5 1.9 %collective-permute-start = (bf16[8,64,128]{2,1,0:T(8,128)(2,1)S(1)}, bf16[8,64,128]{2,1,0:T(8,128)(2,1)S(1)}, u32[]{:S(2)}, u32[]{:S(2)}) collective-permute-start(bf16[8,64,128]{2,1,0:T(8,128)(2,1)S(1)} %get-tuple-element.16), channel_id=1, source_target_pairs={{8,0},{16,8},{24,16},{9,1},{17,9},{25,17},{10,2},{18,10},{26,18},{... | collective-permute-start | bytes 393224 | tf_op jit(solution)/shard_map/ppermute | solution.py:311
  4.4 2.4 %collective-permute-start.1 = (bf16[8,64,128]{2,1,0:T(8,128)(2,1)S(1)}, bf16[8,64,128]{2,1,0:T(8,128)(2,1)S(1)}, u32[]{:S(2)}, u32[]{:S(2)}) collective-permute-start(bf16[8,64,128]{2,1,0:T(8,128)(2,1)S(1)} %get-tuple-element.17), channel_id=1, source_target_pairs={{0,8},{8,16},{16,24},{1,9},{9,17},{17,25},{2,10},{10,18},{18,26},{... | collective-permute-start | bytes 393224 | tf_op jit(solution)/shard_map/ppermute | solution.py:311
  6.9 3.8 %collective-permute-done.1.left_ref = bf16[8,64,128]{2,1,0:T(8,128)(2,1)S(1)} collective-permute-done((bf16[8,64,128]{2,1,0:T(8,128)(2,1)S(1)}, bf16[8,64,128]{2,1,0:T(8,128)(2,1)S(1)}, u32[]{:S(2)}, u32[]{:S(2)}) %collective-permute-start.1) | collective-permute-done | bytes 131104 | tf_op jit(solution)/shard_map/ppermute | solution.py:311
  10.8 2.4 %collective-permute-start.3 = (bf16[16,64,128]{2,1,0:T(8,128)(2,1)S(1)}, bf16[16,64,128]{2,1,0:T(8,128)(2,1)S(1)}, u32[]{:S(2)}, u32[]{:S(2)}) collective-permute-start(bf16[16,64,128]{2,1,0:T(8,128)(2,1)S(1)} %pad_maximum_fusion.1), channel_id=1, source_target_pairs={{1,0},{2,1},{3,2},{4,3},{5,4},{6,5},{7,6},{9,8},{10,9},{11,10},{12... | collective-permute-start | bytes 786440 | tf_op jit(solution)/shard_map/ppermute | solution.py:311
  13.3 4.3 %collective-permute-start.2 = (bf16[16,64,128]{2,1,0:T(8,128)(2,1)S(1)}, bf16[16,64,128]{2,1,0:T(8,128)(2,1)S(1)}, u32[]{:S(2)}, u32[]{:S(2)}) collective-permute-start(bf16[16,64,128]{2,1,0:T(8,128)(2,1)S(1)} %pad_maximum_fusion), channel_id=1, source_target_pairs={{0,1},{1,2},{2,3},{3,4},{4,5},{5,6},{6,7},{8,9},{9,10},{10,11},{11... | collective-permute-start | bytes 786440 | tf_op jit(solution)/shard_map/ppermute | solution.py:311
  17.7 0.2 reshape.15.w1_ref
  18.5 1.6 %collective-permute-done.3.bottom_ref = bf16[16,64,128]{2,1,0:T(8,128)(2,1)S(1)} collective-permute-done((bf16[16,64,128]{2,1,0:T(8,128)(2,1)S(1)}, bf16[16,64,128]{2,1,0:T(8,128)(2,1)S(1)}, u32[]{:S(2)}, u32[]{:S(2)}) %collective-permute-start.3) | collective-permute-done | bytes 262176 | tf_op jit(solution)/shard_map/ppermute | solution.py:311
  20.0 4.8 %collective-permute-done.2.top_ref = bf16[16,64,128]{2,1,0:T(8,128)(2,1)S(1)} collective-permute-done((bf16[16,64,128]{2,1,0:T(8,128)(2,1)S(1)}, bf16[16,64,128]{2,1,0:T(8,128)(2,1)S(1)}, u32[]{:S(2)}, u32[]{:S(2)}) %collective-permute-start.2) | collective-permute-done | bytes 262176 | tf_op jit(solution)/shard_map/ppermute | solution.py:311
  24.9 18.2 %forward.1 = (bf16[64,64,128]{2,1,0:T(8,128)(2,1)S(1)}, f32[80,64,256]{2,1,0:T(8,128)}, f32[64,64,128]{2,1,0:T(8,128)}, bf16[2,65,32,128]{3,2,1,0:T(8,128)(2,1)S(1)}) custom-call(s32[4]{0:T(128)S(1)} %pad_add_fusion.place_ref, bf16[16,64,128]{2,1,0:T(8,128)(2,1)S(1)} %collective-permute-done.2.top_ref, bf16[64,64,128]{2,1,0:T(8,128)(2,1)S(1)} %get-tuple-element.15.main_ref, ...), custom_call_target="tpu_custom_call" | custom-call | tf_op jit(solution)/shard_map/forward/pallas_call | solution.py:373
  43.0 1.2 slice_bitcast_fusion
  44.2 0.2 copy-done.2
  44.4 5.1 %collective-permute-start.4 = (bf16[65,32,128]{2,1,0:T(8,128)(2,1)}, bf16[65,32,128]{2,1,0:T(8,128)(2,1)S(1)}, u32[]{:S(2)}, u32[]{:S(2)}) collective-permute-start(bf16[65,32,128]{2,1,0:T(8,128)(2,1)} %get-tuple-element.26), channel_id=1, source_target_pairs={{0,0},{8,2},{16,4},{24,6},{1,1},{9,3},{17,5},{25,7},{2,8},{10,10},... | collective-permute-start | bytes 1597448 | tf_op jit(solution)/shard_map/ppermute | solution.py:395
  49.9 35.6 %collective-permute-done.4.received_a_ref = bf16[65,32,128]{2,1,0:T(8,128)(2,1)S(1)} collective-permute-done((bf16[65,32,128]{2,1,0:T(8,128)(2,1)}, bf16[65,32,128]{2,1,0:T(8,128)(2,1)S(1)}, u32[]{:S(2)}, u32[]{:S(2)}) %collective-permute-start.4) | collective-permute-done | bytes 532512 | tf_op jit(solution)/shard_map/ppermute | solution.py:395
  85.5 0.8 copy-done.4
  86.3 9.8 %collective-permute-done.5.received_b_ref = bf16[65,32,128]{2,1,0:T(8,128)(2,1)S(1)} collective-permute-done((bf16[65,32,128]{2,1,0:T(8,128)(2,1)}, bf16[65,32,128]{2,1,0:T(8,128)(2,1)S(1)}, u32[]{:S(2)}, u32[]{:S(2)}) %collective-permute-start.5) | collective-permute-done | bytes 532512 | tf_op jit(solution)/shard_map/ppermute | solution.py:395
  96.1 0.8 copy-done.6
  96.9 1.2 copy-done.3
  98.1 1.0 copy-done.5
  99.2 1.0 copy-done.7
  100.2 9.1 %head.1 = (bf16[64,64,128]{2,1,0:T(8,128)(2,1)S(1)}, bf16[8,64,128]{2,1,0:T(8,128)(2,1)S(1)}, bf16[8,64,128]{2,1,0:T(8,128)(2,1)S(1)}) custom-call(s32[4]{0:T(128)S(1)} %pad_add_fusion.place_ref, bf16[65,32,128]{2,1,0:T(8,128)(2,1)S(1)} %copy-done.5, bf16[65,32,128]{2,1,0:T(8,128)(2,1)S(1)} %copy-done.7, bf16[64,64,128]{2,1,0:T(8,128)(2,1)S(1)} %copy-done.3, ...), custom_call_target="tpu_custom_call" | custom-call | tf_op jit(solution)/shard_map/head/pallas_call | solution.py:401
  109.4 1.9 %collective-permute-start.6 = (bf16[8,64,128]{2,1,0:T(8,128)(2,1)S(1)}, bf16[8,64,128]{2,1,0:T(8,128)(2,1)S(1)}, u32[]{:S(2)}, u32[]{:S(2)}) collective-permute-start(bf16[8,64,128]{2,1,0:T(8,128)(2,1)S(1)} %get-tuple-element.22), channel_id=1, source_target_pairs={{8,0},{16,8},{24,16},{9,1},{17,9},{25,17},{10,2},{18,10},{26,18},{... | collective-permute-start | bytes 393224 | tf_op jit(solution)/shard_map/ppermute | solution.py:311
  111.3 2.4 %collective-permute-start.7 = (bf16[8,64,128]{2,1,0:T(8,128)(2,1)S(1)}, bf16[8,64,128]{2,1,0:T(8,128)(2,1)S(1)}, u32[]{:S(2)}, u32[]{:S(2)}) collective-permute-start(bf16[8,64,128]{2,1,0:T(8,128)(2,1)S(1)} %get-tuple-element.23), channel_id=1, source_target_pairs={{0,8},{8,16},{16,24},{1,9},{9,17},{17,25},{2,10},{10,18},{18,26},{... | collective-permute-start | bytes 393224 | tf_op jit(solution)/shard_map/ppermute | solution.py:311
  113.8 3.8 %collective-permute-done.7.left_ref = bf16[8,64,128]{2,1,0:T(8,128)(2,1)S(1)} collective-permute-done((bf16[8,64,128]{2,1,0:T(8,128)(2,1)S(1)}, bf16[8,64,128]{2,1,0:T(8,128)(2,1)S(1)}, u32[]{:S(2)}, u32[]{:S(2)}) %collective-permute-start.7) | collective-permute-done | bytes 131104 | tf_op jit(solution)/shard_map/ppermute | solution.py:311
  117.6 4.2 %collective-permute-start.9 = (bf16[16,64,128]{2,1,0:T(8,128)(2,1)S(1)}, bf16[16,64,128]{2,1,0:T(8,128)(2,1)S(1)}, u32[]{:S(2)}, u32[]{:S(2)}) collective-permute-start(bf16[16,64,128]{2,1,0:T(8,128)(2,1)S(1)} %pad_maximum_fusion.3), channel_id=1, source_target_pairs={{1,0},{2,1},{3,2},{4,3},{5,4},{6,5},{7,6},{9,8},{10,9},{11,10},{12... | collective-permute-start | bytes 786440 | tf_op jit(solution)/shard_map/ppermute | solution.py:311
  121.9 2.5 %collective-permute-start.8 = (bf16[16,64,128]{2,1,0:T(8,128)(2,1)S(1)}, bf16[16,64,128]{2,1,0:T(8,128)(2,1)S(1)}, u32[]{:S(2)}, u32[]{:S(2)}) collective-permute-start(bf16[16,64,128]{2,1,0:T(8,128)(2,1)S(1)} %pad_maximum_fusion.2), channel_id=1, source_target_pairs={{0,1},{1,2},{2,3},{3,4},{4,5},{5,6},{6,7},{8,9},{9,10},{10,11},{11... | collective-permute-start | bytes 786440 | tf_op jit(solution)/shard_map/ppermute | solution.py:311
  124.4 0.2 copy.25
  124.8 0.2 copy.26
  125.1 1.8 %collective-permute-done.9.bottom_ref = bf16[16,64,128]{2,1,0:T(8,128)(2,1)S(1)} collective-permute-done((bf16[16,64,128]{2,1,0:T(8,128)(2,1)S(1)}, bf16[16,64,128]{2,1,0:T(8,128)(2,1)S(1)}, u32[]{:S(2)}, u32[]{:S(2)}) %collective-permute-start.9) | collective-permute-done | bytes 262176 | tf_op jit(solution)/shard_map/ppermute | solution.py:311
  126.9 5.1 %collective-permute-done.8.top_ref = bf16[16,64,128]{2,1,0:T(8,128)(2,1)S(1)} collective-permute-done((bf16[16,64,128]{2,1,0:T(8,128)(2,1)S(1)}, bf16[16,64,128]{2,1,0:T(8,128)(2,1)S(1)}, u32[]{:S(2)}, u32[]{:S(2)}) %collective-permute-start.8) | collective-permute-done | bytes 262176 | tf_op jit(solution)/shard_map/ppermute | solution.py:311
  132.0 19.4 %backward.1 = f32[4096,128]{1,0:T(8,128)} custom-call(bf16[16,64,128]{2,1,0:T(8,128)(2,1)S(1)} %collective-permute-done.8.top_ref, bf16[64,64,128]{2,1,0:T(8,128)(2,1)S(1)} %get-tuple-element.21.main_ref, bf16[8,64,128]{2,1,0:T(8,128)(2,1)S(1)} %collective-permute-done.6.right_ref, bf16[8,64,128]{2,1,0:T(8,128)(2,1)S(1)} %collective-permute-done.7.left_ref, ...), custom_call_target="tpu_custom_call" | custom-call | tf_op jit(solution)/shard_map/backward/pallas_call | solution.py:416
  (52 shorter events, 1.8 us)
Async XLA Ops:
  0.0 1.2 copy-start.1
  1.2 16.4 %copy-start.10 = (bf16[3,3,64,64]{3,2,1,0:T(8,128)(2,1)S(1)}, bf16[3,3,64,64]{3,2,1,0:T(8,128)(2,1)}, u32[]{:S(2)}) copy-start(bf16[3,3,64,64]{3,2,1,0:T(8,128)(2,1)} %param.9) | copy-start | bytes 221188
  1.2 16.7 %copy-start.9 = (bf16[3,3,64,64]{3,2,1,0:T(8,128)(2,1)S(1)}, bf16[3,3,64,64]{3,2,1,0:T(8,128)(2,1)}, u32[]{:S(2)}) copy-start(bf16[3,3,64,64]{3,2,1,0:T(8,128)(2,1)} %param.11) | copy-start | bytes 221188
  1.2 17.0 %copy-start.12 = (f32[64]{0:T(128)S(1)}, f32[64]{0:T(128)}, u32[]{:S(2)}) copy-start(f32[64]{0:T(128)} %param.10) | copy-start | bytes 772
  1.2 17.1 %copy-start.13 = (f32[64]{0:T(128)S(1)}, f32[64]{0:T(128)}, u32[]{:S(2)}) copy-start(f32[64]{0:T(128)} %param.12) | copy-start | bytes 772
  1.2 23.6 %copy-start.8 = (s32[64,128]{1,0:T(8,128)S(1)}, s32[64,128]{1,0:T(8,128)}, u32[]{:S(2)}) copy-start(s32[64,128]{1,0:T(8,128)} %target_ref.3) | copy-start | bytes 98308
  2.5 4.4 %collective-permute-start = (bf16[8,64,128]{2,1,0:T(8,128)(2,1)S(1)}, bf16[8,64,128]{2,1,0:T(8,128)(2,1)S(1)}, u32[]{:S(2)}, u32[]{:S(2)}) collective-permute-start(bf16[8,64,128]{2,1,0:T(8,128)(2,1)S(1)} %get-tuple-element.16), channel_id=1, source_target_pairs={{8,0},{16,8},{24,16},{9,1},{17,9},{25,17},{10,2},{18,10},{26,18},{... | collective-permute-start | bytes 393224 | tf_op jit(solution)/shard_map/ppermute | solution.py:311
  4.4 6.3 %collective-permute-start.1 = (bf16[8,64,128]{2,1,0:T(8,128)(2,1)S(1)}, bf16[8,64,128]{2,1,0:T(8,128)(2,1)S(1)}, u32[]{:S(2)}, u32[]{:S(2)}) collective-permute-start(bf16[8,64,128]{2,1,0:T(8,128)(2,1)S(1)} %get-tuple-element.17), channel_id=1, source_target_pairs={{0,8},{8,16},{16,24},{1,9},{9,17},{17,25},{2,10},{10,18},{18,26},{... | collective-permute-start | bytes 393224 | tf_op jit(solution)/shard_map/ppermute | solution.py:311
  10.8 9.3 %collective-permute-start.3 = (bf16[16,64,128]{2,1,0:T(8,128)(2,1)S(1)}, bf16[16,64,128]{2,1,0:T(8,128)(2,1)S(1)}, u32[]{:S(2)}, u32[]{:S(2)}) collective-permute-start(bf16[16,64,128]{2,1,0:T(8,128)(2,1)S(1)} %pad_maximum_fusion.1), channel_id=1, source_target_pairs={{1,0},{2,1},{3,2},{4,3},{5,4},{6,5},{7,6},{9,8},{10,9},{11,10},{12... | collective-permute-start | bytes 786440 | tf_op jit(solution)/shard_map/ppermute | solution.py:311
  13.3 11.6 %collective-permute-start.2 = (bf16[16,64,128]{2,1,0:T(8,128)(2,1)S(1)}, bf16[16,64,128]{2,1,0:T(8,128)(2,1)S(1)}, u32[]{:S(2)}, u32[]{:S(2)}) collective-permute-start(bf16[16,64,128]{2,1,0:T(8,128)(2,1)S(1)} %pad_maximum_fusion), channel_id=1, source_target_pairs={{0,1},{1,2},{2,3},{3,4},{4,5},{5,6},{6,7},{8,9},{9,10},{10,11},{11... | collective-permute-start | bytes 786440 | tf_op jit(solution)/shard_map/ppermute | solution.py:311
  18.5 31.1 %copy-start.11 = (bf16[37,64]{1,0:T(8,128)(2,1)S(1)}, bf16[37,64]{1,0:T(8,128)(2,1)}, u32[]{:S(2)}) copy-start(bf16[37,64]{1,0:T(8,128)(2,1)} %param.13) | copy-start | bytes 14212
  18.5 31.3 %copy-start.14 = (f32[37]{0:T(128)S(1)}, f32[37]{0:T(128)}, u32[]{:S(2)}) copy-start(f32[37]{0:T(128)} %param.14) | copy-start | bytes 448
  43.0 1.3 copy-start.2
  43.0 53.9 %copy-start = (f32[64,64,128]{2,1,0:T(8,128)S(1)}, f32[64,64,128]{2,1,0:T(8,128)}, u32[]{:S(2)}) copy-start(f32[64,64,128]{2,1,0:T(8,128)} %get-tuple-element.20.slope_two_ref) | copy-start | bytes 6291460
  44.4 41.1 %collective-permute-start.4 = (bf16[65,32,128]{2,1,0:T(8,128)(2,1)}, bf16[65,32,128]{2,1,0:T(8,128)(2,1)S(1)}, u32[]{:S(2)}, u32[]{:S(2)}) collective-permute-start(bf16[65,32,128]{2,1,0:T(8,128)(2,1)} %get-tuple-element.26), channel_id=1, source_target_pairs={{0,0},{8,2},{16,4},{24,6},{1,1},{9,3},{17,5},{25,7},{2,8},{10,10},... | collective-permute-start | bytes 1597448 | tf_op jit(solution)/shard_map/ppermute | solution.py:395
  49.5 46.6 %collective-permute-start.5 = (bf16[65,32,128]{2,1,0:T(8,128)(2,1)}, bf16[65,32,128]{2,1,0:T(8,128)(2,1)S(1)}, u32[]{:S(2)}, u32[]{:S(2)}) collective-permute-start(bf16[65,32,128]{2,1,0:T(8,128)(2,1)} %get-tuple-element.25), channel_id=1, source_target_pairs={{0,1},{8,3},{16,5},{24,7},{1,0},{9,2},{17,4},{25,6},{2,9},{10,11},... | collective-permute-start | bytes 1597448 | tf_op jit(solution)/shard_map/ppermute | solution.py:395
  85.5 0.8 copy-start.4
  96.1 0.8 copy-start.6
  96.9 1.2 copy-start.3
  98.1 1.0 copy-start.5
  99.2 1.0 copy-start.7
  109.4 4.4 %collective-permute-start.6 = (bf16[8,64,128]{2,1,0:T(8,128)(2,1)S(1)}, bf16[8,64,128]{2,1,0:T(8,128)(2,1)S(1)}, u32[]{:S(2)}, u32[]{:S(2)}) collective-permute-start(bf16[8,64,128]{2,1,0:T(8,128)(2,1)S(1)} %get-tuple-element.22), channel_id=1, source_target_pairs={{8,0},{16,8},{24,16},{9,1},{17,9},{25,17},{10,2},{18,10},{26,18},{... | collective-permute-start | bytes 393224 | tf_op jit(solution)/shard_map/ppermute | solution.py:311
  111.3 6.3 %collective-permute-start.7 = (bf16[8,64,128]{2,1,0:T(8,128)(2,1)S(1)}, bf16[8,64,128]{2,1,0:T(8,128)(2,1)S(1)}, u32[]{:S(2)}, u32[]{:S(2)}) collective-permute-start(bf16[8,64,128]{2,1,0:T(8,128)(2,1)S(1)} %get-tuple-element.23), channel_id=1, source_target_pairs={{0,8},{8,16},{16,24},{1,9},{9,17},{17,25},{2,10},{10,18},{18,26},{... | collective-permute-start | bytes 393224 | tf_op jit(solution)/shard_map/ppermute | solution.py:311
  117.6 9.3 %collective-permute-start.9 = (bf16[16,64,128]{2,1,0:T(8,128)(2,1)S(1)}, bf16[16,64,128]{2,1,0:T(8,128)(2,1)S(1)}, u32[]{:S(2)}, u32[]{:S(2)}) collective-permute-start(bf16[16,64,128]{2,1,0:T(8,128)(2,1)S(1)} %pad_maximum_fusion.3), channel_id=1, source_target_pairs={{1,0},{2,1},{3,2},{4,3},{5,4},{6,5},{7,6},{9,8},{10,9},{11,10},{12... | collective-permute-start | bytes 786440 | tf_op jit(solution)/shard_map/ppermute | solution.py:311
  121.9 10.1 %collective-permute-start.8 = (bf16[16,64,128]{2,1,0:T(8,128)(2,1)S(1)}, bf16[16,64,128]{2,1,0:T(8,128)(2,1)S(1)}, u32[]{:S(2)}, u32[]{:S(2)}) collective-permute-start(bf16[16,64,128]{2,1,0:T(8,128)(2,1)S(1)} %pad_maximum_fusion.2), channel_id=1, source_target_pairs={{0,1},{1,2},{2,3},{3,4},{4,5},{5,6},{6,7},{8,9},{9,10},{10,11},{11... | collective-permute-start | bytes 786440 | tf_op jit(solution)/shard_map/ppermute | solution.py:311
where the time goes:
time: 152 us; the launch traced here: 151 us
  waiting for transfers between devices  66.3 us (44%)
  Pallas kernels  48 us (32%)
  starting transfers between devices  27.3 us (18%)
  local copies, waits for them, and re-layouts  9.34 us (6%)
    ppermute x2, waiting for transfers between devices, local(): lax.ppermute(sent[k], ('row', 'col'), mirror_pairs(k))  45.4 us
    ppermute x8, starting transfers between devices, shifted(): return lax.ppermute(tensor, axis, pairs)  22.1 us
    ppermute x8, waiting for transfers between devices, shifted(): return lax.ppermute(tensor, axis, pairs)  20.9 us
    pallas_call x1, Pallas kernels, local(): pl.pallas_call(backward_kernel, out_shape=jax.ShapeDtypeStruct((channels...  19.4 us
    pallas_call x1, Pallas kernels, local(): pl.pallas_call(forward_kernel, out_shape=(row_type, jax.ShapeDtypeStruct(...  18.2 us
    pallas_call x1, Pallas kernels, local(): pl.pallas_call(head_kernel, out_shape=(row_type, pack_type, pack_type), i...  9.14 us
    unnamed x32, local copies, waits for them, and re-layouts  6.53 us
    ppermute x2, starting transfers between devices, local(): lax.ppermute(sent[k], ('row', 'col'), mirror_pairs(k))  5.15 us
  transfers between devices with their start and end apart: 10, of which 8 were waited for; matrix products, arithmetic and copies ran while one was open for 1% of the time, Pallas kernels for 0%

commit v1 on v0

v1 whole, which is shorter than its diff:
```python
import jax
import jax.numpy as jnp
from jax import lax
from jax.experimental import pallas as pl
from jax.experimental.pallas import tpu as pltpu
from jax.sharding import PartitionSpec as P

DILATION_FIRST = 4
DILATION_SECOND = 8
MARGIN = DILATION_FIRST + DILATION_SECOND
SLOT = 16
F32 = jnp.float32
BF16 = jnp.bfloat16
VMEM = pl.BlockSpec(memory_space=pltpu.VMEM)
SMEM = pl.BlockSpec(memory_space=pltpu.SMEM)


def params(megabytes):
    return pltpu.CompilerParams(vmem_limit_bytes=megabytes << 20)


def lanes_of(shape):
    return lax.broadcasted_iota(jnp.int32, shape, len(shape) - 1)


def pack_edges(rows, first_ref, second_ref, block):
    count = len(rows)
    width = rows[0].shape[-1]
    slot = lanes_of(rows[0].shape) // SLOT
    first = second = None
    for i, row in enumerate(rows):
        turned = pltpu.roll(row, SLOT * i, 1) if i else row
        first = turned if first is None else jnp.where(slot == i, turned, first)
        second = turned if second is None else jnp.where(slot == (i - 1) % count, turned, second)
    first_ref[block] = first.astype(BF16)
    second_ref[block] = second.astype(BF16)


def ring_row(main, right, left, i):
    width = main.shape[-1]
    lane = lanes_of(main.shape)
    both = jnp.where(lane // SLOT == i, right.astype(F32), left.astype(F32))
    if i:
        both = pltpu.roll(both, width - SLOT * i, 1)
    edge = jnp.where((lane < MARGIN) | (lane >= width - MARGIN), both, 0.0)
    return jnp.concatenate([main, edge.astype(BF16)], axis=1)


def strip_ring(strip_ref, slots, ring_ref):
    per = ring_ref.shape[-1] // 2 // SLOT
    near = -(-MARGIN // per)
    for e in range(MARGIN):
        block, slot = divmod(e + slots, per)
        right, left = strip_ref[MARGIN + block], strip_ref[MARGIN + near + block]
        ring_ref[e] = ring_row(strip_ref[e], right, left, slot)


def main_ring(main_ref, right_ref, left_ref, ring_ref):
    per = main_ref.shape[-1] // SLOT

    @pl.loop(0, main_ref.shape[0] // per)
    def _(block):
        right = right_ref[block]
        left = left_ref[block]
        for slot in range(per):
            row = block * per + slot
            ring_ref[row] = ring_row(main_ref[row], right, left, slot)


def taps(row, spacing, width):
    wide = row.astype(F32)
    full = row.shape[-1]
    back = pltpu.roll(wide, spacing, 1)[:, :width]
    ahead = pltpu.roll(wide, full - spacing, 1)[:, :width]
    return jnp.concatenate([back.astype(BF16), row[:, :width], ahead.astype(BF16)], axis=0)


def wide_unit(source_ref, spacing):
    def unit(e):
        row = source_ref[e]
        return taps(row, spacing, row.shape[-1]), row.astype(F32)

    return unit


def narrow_unit(source_ref, spacing):
    width = source_ref.shape[-1] // 2

    def unit(e):
        rows = [source_ref[2 * e + k] for k in range(2)]
        both = jnp.concatenate([taps(row, spacing, width) for row in rows], axis=1)
        return both, jnp.concatenate([row[:, :width] for row in rows], axis=1).astype(F32)

    return unit


def inner_conv(unit, count, weights, reach, sums_ref, finish, unroll):
    channels = weights.shape[0] // 3

    def step(e, kind):
        seen, own = unit(e)
        z = jnp.dot(weights, seen, preferred_element_type=F32)
        middle, behind = z[channels : 2 * channels] + own, z[2 * channels :]
        if kind == 0:
            sums_ref[e] = behind
            sums_ref[e + reach] = middle
        else:
            total = sums_ref[e] + behind
            if kind == 1:
                sums_ref[e] = total
            else:
                finish(e - 2 * reach, total)
            sums_ref[e + reach] += middle
        sums_ref[e + 2 * reach] = z[:channels]

    for kind, begin, end in ((0, 0, reach), (1, reach, 2 * reach), (2, 2 * reach, count)):
        many = max(k for k in range(1, unroll + 1) if (end - begin) % k == 0)

        @pl.loop(begin, end, step=many)
        def _(e):
            for k in range(many):
                step(e + k, kind)


def keep_sums(sums_ref, count, reach, kept_ref):
    for k in range(2 * reach):
        kept_ref[0, k] = sums_ref[k]
        kept_ref[1, k] = sums_ref[count + k]


def edge_conv(unit, count, weights, reach, below, kept_ref, parts_ref, finish):
    channels = weights.shape[0] // 3
    for k in range(count):
        seen, own = unit(k)
        if below:
            taken = [t for t in range(3) if k + (2 - t) * reach < count]
        else:
            taken = [t for t in range(3) if k - t * reach >= 0]
        z = jnp.dot(
            weights[channels * taken[0] : channels * (taken[-1] + 1)],
            seen,
            preferred_element_type=F32,
        )
        for i, t in enumerate(taken):
            part = z[channels * i : channels * (i + 1)]
            parts_ref[k, t] = part + own if t == 1 else part
    for i in range(count):
        if below:
            total = parts_ref[i, 2]
            others = [(i - (2 - t) * reach, t) for t in range(2)]
            kept = i
        else:
            total = parts_ref[i, 0]
            others = [(i + t * reach, t) for t in (1, 2)]
            kept = i - count + 2 * reach
        for k, t in others:
            if 0 <= k < count:
                total = total + parts_ref[k, t]
        if 0 <= kept < 2 * reach:
            total = total + kept_ref[int(below), kept]
        finish(i, total)


def activated(pre):
    decay = jnp.exp(jnp.minimum(pre, 0.0))
    up = pre > 0
    return jnp.where(up, pre, decay - 1.0), jnp.where(up, 1.0, decay)


def lanes_inside(place_ref, width):
    lane = lanes_of((1, 2 * width))
    q = jnp.where(lane < width + width // 2, lane, lane - 2 * width) + place_ref[1] * width
    return jnp.where((q >= 0) & (q < place_ref[3] * width), 1.0, 0.0)


def put_piece(send_refs, mine, p, hidden):
    channels, width = hidden.shape
    lo, hi = hidden[: channels // 2], hidden[channels // 2 :]
    low = lanes_of(lo.shape) < width // 2
    first = jnp.where(low, lo, pltpu.roll(hi, width // 2, 1)).astype(BF16)
    second = jnp.where(low, pltpu.roll(lo, width // 2, 1), hi).astype(BF16)
    swap = mine == 1
    send_refs[0][p] = jnp.where(swap, second, first)
    send_refs[1][p] = jnp.where(swap, first, second)


def prepare_kernel(x_ref, xt_ref, first_ref, second_ref):
    channels, size, width = x_ref.shape
    per = width // SLOT

    @pl.loop(0, size // per)
    def _(block):
        chunk = x_ref[:, pl.ds(block * per, per), :].astype(F32)
        turned = jnp.swapaxes(chunk, 0, 1)
        xt_ref[pl.ds(block * per, per)] = turned.astype(BF16)
        pack_edges([turned[i] for i in range(per)], first_ref, second_ref, block)


def forward_inner_kernel(
    place_ref, main_ref, right_ref, left_ref, target_ref, w1_ref, b1_ref, w2_ref, b2_ref,
    kept_one_ref, kept_two_ref, hidden_ref, slope_one_ref, slope_two_ref, send_a_ref, send_b_ref,
    ring_ref, near_ref, sums_ref,
):
    size, channels, width = main_ref.shape
    d1, d2 = DILATION_FIRST, DILATION_SECOND
    main_ring(main_ref, right_ref, left_ref, ring_ref)
    lane_ok = lanes_inside(place_ref, width)
    mine = lax.rem(place_ref[0], width // size)
    b1 = b1_ref[...]
    b2 = b2_ref[...]

    def finish_one(i, total):
        hidden, slope = activated(total + b1)
        near_ref[i] = (hidden * lane_ok).astype(BF16)
        slope_one_ref[i] = slope * lane_ok

    inner_conv(wide_unit(ring_ref, d1), size, w1_ref[...], d1, sums_ref, finish_one, 8)
    keep_sums(sums_ref, size, d1, kept_one_ref)

    def finish_two(i, total):
        hidden, slope = activated(total + b2)
        for k in range(2):
            own = hidden[:, k * width : (k + 1) * width]
            hidden_ref[2 * i + k] = own.astype(BF16)
            slope_two_ref[2 * i + k] = slope[:, k * width : (k + 1) * width]
            put_piece((send_a_ref, send_b_ref), mine, 2 * i + k, own)

    count = near_ref.shape[0] // 2
    inner_conv(narrow_unit(near_ref, d2), count, w2_ref[...], d2 // 2, sums_ref, finish_two, 10)
    keep_sums(sums_ref, count, d2 // 2, kept_two_ref)
    put_piece((send_a_ref, send_b_ref), mine, size - 2 * MARGIN, target_ref[...].astype(F32))


def forward_edge_kernel(
    place_ref, top_ref, bottom_ref, kept_one_ref, kept_two_ref, w1_ref, b1_ref, w2_ref, b2_ref,
    hidden_ref, slope_one_ref, slope_two_ref, send_a_ref, send_b_ref,
    ring_ref, near_ref, parts_ref,
):
    width = hidden_ref.shape[-1]
    size = width // 2
    d1, d2 = DILATION_FIRST, DILATION_SECOND
    lane_ok = lanes_inside(place_ref, width)
    mine = lax.rem(place_ref[0], width // size)
    b1 = b1_ref[...]
    b2 = b2_ref[...]
    w1 = w1_ref[...]
    w2 = w2_ref[...]
    for below, strip_ref in enumerate((top_ref, bottom_ref)):
        ring, near = ring_ref.at[below], near_ref.at[below]
        parts = parts_ref.at[below]
        strip_ring(strip_ref, 0 if below else -MARGIN % (width // SLOT), ring)

        def finish_one(i, total):
            hidden, slope = activated(total + b1)
            p = (size - d1 if below else d1 - MARGIN) + i + place_ref[0] * size
            ok = lane_ok * jnp.where((p >= 0) & (p < place_ref[2] * size), 1.0, 0.0)
            near[i] = (hidden * ok).astype(BF16)
            slope_one_ref[below, i] = slope * ok

        edge_conv(
            wide_unit(ring, d1), MARGIN, w1, d1, below, kept_one_ref, parts, finish_one
        )

        def finish_two(i, total):
            hidden, slope = activated(total + b2)
            for k in range(2):
                row = below * MARGIN + 2 * i + k
                own = hidden[:, k * width : (k + 1) * width]
                hidden_ref[row] = own.astype(BF16)
                slope_two_ref[row] = slope[:, k * width : (k + 1) * width]
                put_piece((send_a_ref, send_b_ref), mine, row, own)

        edge_conv(
            narrow_unit(near, d2), MARGIN // 2, w2, d2 // 2, below, kept_two_ref, parts, finish_two
        )


def head_kernel(
    place_ref, inner_a_ref, inner_b_ref, edge_a_ref, edge_b_ref,
    hidden_inner_ref, hidden_edge_ref, slope_inner_ref, slope_edge_ref, target_ref,
    weight_ref, weight_t_ref, bias_ref,
    delta_ref, first_ref, second_ref,
    wide_ref, turned_ref, target_t_ref,
):
    size, channels, width = delta_ref.shape
    half = channels // 2
    group = width // size
    mine = lax.rem(place_ref[0], group)
    inner = size - 2 * MARGIN

    def widen(source_a_ref, source_b_ref, row, p):
        wide_ref[pl.ds((mine * size + p) * half, half), :] = source_a_ref[row].astype(F32)
        wide_ref[pl.ds(((1 - mine) * size + p) * half, half), :] = source_b_ref[row].astype(F32)

    for k in range(inner):
        widen(inner_a_ref, inner_b_ref, k, k + MARGIN)
    for k in range(MARGIN):
        widen(edge_a_ref, edge_b_ref, k, k)
        widen(edge_a_ref, edge_b_ref, MARGIN + k, MARGIN + inner + k)

    @pl.loop(0, half, step=8)
    def _(c):
        for k in range(8):
            page = wide_ref[pl.ds(c + k, width, stride=half), :]
            page = page.T
            turned_ref[pl.ds(c + k, size, stride=channels), :] = page[:size]
            turned_ref[pl.ds(c + k + half, size, stride=channels), :] = page[size:]

    label_a = inner_a_ref[inner].astype(F32)
    label_b = inner_b_ref[inner].astype(F32)
    label_0 = jnp.where(mine == 0, label_a, label_b)
    label_1 = jnp.where(mine == 0, label_b, label_a)
    page = jnp.concatenate(
        [label_0, pltpu.roll(label_0, size, 1), label_1, pltpu.roll(label_1, size, 1)], axis=0
    )
    target_t_ref[...] = page.T[:size].astype(jnp.int32)

    bins = weight_ref.shape[0]
    weight = weight_ref[...]
    weight_t = weight_t_ref[...]
    bias = bias_ref[...]
    bin_id = lax.broadcasted_iota(jnp.int32, (bins, 2 * width), 0)
    per = width // SLOT

    def own(p, inner_ref, edge_ref):
        if p < MARGIN:
            return edge_ref[p]
        return inner_ref[p - MARGIN] if p < MARGIN + inner else edge_ref[p - inner]

    def pair(p):
        symmetric = jnp.concatenate(
            [
                (
                    own(p + k, hidden_inner_ref, hidden_edge_ref).astype(F32)
                    + turned_ref[pl.ds((p + k) * channels, channels), :]
                ).astype(BF16)
                for k in range(2)
            ],
            axis=1,
        )
        logits = jnp.dot(weight, symmetric, preferred_element_type=F32) + bias
        top = jnp.max(logits, axis=0, keepdims=True)
        raised = jnp.exp(logits - top)
        probability = raised / jnp.sum(raised, axis=0, keepdims=True)
        labels = [
            jnp.concatenate([ref[pl.ds(p + k, 1), :] for k in range(2)], axis=1)
            for ref in (target_ref, target_t_ref)
        ]
        grads = [
            (probability - jnp.where(bin_id == label, 1.0, 0.0)).astype(BF16).astype(F32)
            for label in labels
        ]
        bins_sum = (grads[0] + grads[1]).astype(BF16)
        grad_two = jnp.dot(weight_t, bins_sum, preferred_element_type=F32)
        return [
            (
                grad_two[:, k * width : (k + 1) * width]
                * own(p + k, slope_inner_ref, slope_edge_ref)
            ).astype(BF16)
            for k in range(2)
        ]

    for block in range(size // per):
        deltas = []
        for k in range(0, per, 2):
            deltas += pair(block * per + k)
        for k in range(per):
            delta_ref[block * per + k] = deltas[k]
        pack_edges([d.astype(F32) for d in deltas], first_ref, second_ref, block)


def backward_inner_kernel(
    main_ref, right_ref, left_ref, slope_one_ref, w2_ref, w1_ref,
    kept_two_ref, kept_one_ref, rows_ref,
    ring_ref, near_ref, sums_ref,
):
    size, channels, width = main_ref.shape
    d1, d2 = DILATION_FIRST, DILATION_SECOND
    main_ring(main_ref, right_ref, left_ref, ring_ref)

    def finish_one(i, total):
        near_ref[i] = (total * slope_one_ref[i + d2 - d1]).astype(BF16)

    inner_conv(wide_unit(ring_ref, d2), size, w2_ref[...], d2, sums_ref, finish_one, 8)
    keep_sums(sums_ref, size, d2, kept_two_ref)

    def finish_two(i, total):
        for k in range(2):
            rows_ref[2 * i + k] = total[:, k * width : (k + 1) * width]

    count = near_ref.shape[0] // 2
    inner_conv(narrow_unit(near_ref, d1), count, w1_ref[...], d1 // 2, sums_ref, finish_two, 10)
    keep_sums(sums_ref, count, d1 // 2, kept_one_ref)


def backward_edge_kernel(
    top_ref, bottom_ref, kept_two_ref, kept_one_ref, rows_ref, slope_inner_ref, slope_edge_ref,
    w2_ref, w1_ref,
    out_ref,
    ring_ref, near_ref, parts_ref,
):
    inner, channels, width = rows_ref.shape
    size = inner + 2 * MARGIN
    d1, d2 = DILATION_FIRST, DILATION_SECOND
    w2 = w2_ref[...]
    w1 = w1_ref[...]

    def put(p, row):
        out_ref[pl.ds(p, channels, stride=size), :] = row

    for k in range(inner):
        put(k + MARGIN, rows_ref[k])
    for below, strip_ref in enumerate((top_ref, bottom_ref)):
        ring, near = ring_ref.at[below], near_ref.at[below]
        parts = parts_ref.at[below]
        strip_ring(strip_ref, 0 if below else -MARGIN % (width // SLOT), ring)

        def finish_one(i, total):
            p = (size - d2 if below else d2 - MARGIN) + i
            if d1 <= p < size - d1:
                slope = slope_inner_ref[p - d1]
            else:
                slope = slope_edge_ref[below, p - (size - d1 if below else d1 - MARGIN)]
            near[i] = (total * slope).astype(BF16)

        edge_conv(
            wide_unit(ring, d2), MARGIN, w2, d2, below, kept_two_ref, parts, finish_one
        )

        def finish_two(i, total):
            for k in range(2):
                p = below * (size - MARGIN) + 2 * i + k
                put(p, total[:, k * width : (k + 1) * width])

        edge_conv(
            narrow_unit(near, d1), MARGIN // 2, w1, d1 // 2, below, kept_one_ref, parts, finish_two
        )


def shifted(tensor, axis, step):
    count = lax.axis_size(axis)
    pairs = [(i, i + step) for i in range(count) if 0 <= i + step < count]
    return lax.ppermute(tensor, axis, pairs)


def strips(main, right, left):
    near = -(-MARGIN // (main.shape[-1] // SLOT))
    top = shifted(jnp.concatenate([main[-MARGIN:], right[-near:], left[-near:]]), "col", 1)
    bottom = shifted(jnp.concatenate([main[:MARGIN], right[:near], left[:near]]), "col", -1)
    return top, bottom


def mirror_pairs(step):
    col_count, row_count = lax.axis_size("col"), lax.axis_size("row")
    group = col_count // row_count
    return [
        (r * col_count + c, (c // group) * col_count + group * r + (c % group + step) % group)
        for c in range(col_count)
        for r in range(row_count)
    ]


def local(
    pair_features,
    first_block_kernel,
    first_block_bias,
    second_block_kernel,
    second_block_bias,
    head_weight,
    head_bias,
    target,
):
    channels, size, width = pair_features.shape
    d1, d2 = DILATION_FIRST, DILATION_SECOND
    per = width // SLOT
    place = jnp.stack(
        [
            lax.axis_index("col"), lax.axis_index("row"),
            jnp.int32(lax.axis_size("col")), jnp.int32(lax.axis_size("row")),
        ]
    ).astype(jnp.int32)

    def ahead(kernel):
        return kernel.transpose(0, 2, 1, 3).reshape(3 * channels, 3 * channels)

    def back(kernel):
        return kernel[::-1, ::-1].transpose(0, 3, 1, 2).reshape(3 * channels, 3 * channels)

    def rows(count, lanes=width, kind=BF16):
        return jax.ShapeDtypeStruct((count, channels, lanes), kind)

    def sides(count, lanes=2 * width):
        return jax.ShapeDtypeStruct((2, count, channels, lanes), F32)

    def pieces(count):
        return jax.ShapeDtypeStruct((count, channels // 2, width), BF16)

    def call(kernel, name, outs, scratch, megabytes, flops, *operands):
        places = [SMEM if operand is place else VMEM for operand in operands]
        return pl.pallas_call(
            kernel,
            out_shape=outs,
            in_specs=places,
            out_specs=jax.tree.map(lambda _: VMEM, outs),
            scratch_shapes=[pltpu.VMEM(shape, kind) for shape, kind in scratch],
            compiler_params=params(megabytes),
            cost_estimate=pl.CostEstimate(flops=flops, bytes_accessed=8 << 20, transcendentals=0),
            name=name,
        )(*operands)

    inner = size - 2 * MARGIN
    ring = (channels, 2 * width)
    parts = ((2, MARGIN, 3) + ring, F32)
    edge_rings = [((2, MARGIN) + ring, BF16), ((2, MARGIN) + ring, BF16), parts]
    macs = 9 * channels * channels * size * width

    packs = rows(size // per)
    main, first, second = call(
        prepare_kernel, "prepare", (rows(size), packs, packs), [], 24, 1, pair_features
    )
    right, left = shifted(first, "row", -1), shifted(second, "row", 1)
    top, bottom = strips(main, right, left)
    w1, w2 = ahead(first_block_kernel), ahead(second_block_kernel)
    b1, b2 = first_block_bias[:, None], second_block_bias[:, None]
    kept_one, kept_two, hidden_inner, slope_one_inner, slope_two_inner, *sent_inner = call(
        forward_inner_kernel,
        "forward_inner",
        (
            sides(2 * d1), sides(d2), rows(inner), rows(size - 2 * d1, 2 * width, F32),
            rows(inner, width, F32), pieces(inner + 1), pieces(inner + 1),
        ),
        [
            ((size,) + ring, BF16), ((size - 2 * d1,) + ring, BF16),
            ((size + 2 * d1,) + ring, F32),
        ],
        32, 8 * macs, place, main, right, left, target, w1, b1, w2, b2,
    )
    got_inner = [lax.ppermute(sent_inner[k], ("row", "col"), mirror_pairs(k)) for k in range(2)]
    hidden_edge, slope_one_edge, slope_two_edge, *sent_edge = call(
        forward_edge_kernel,
        "forward_edge",
        (
            rows(2 * MARGIN), sides(MARGIN), rows(2 * MARGIN, width, F32),
            pieces(2 * MARGIN), pieces(2 * MARGIN),
        ),
        edge_rings,
        32, 4 * macs, place, top, bottom, kept_one, kept_two, w1, b1, w2, b2,
    )
    got_edge = [lax.ppermute(sent_edge[k], ("row", "col"), mirror_pairs(k)) for k in range(2)]

    bins = head_weight.shape[0]
    bins_up = -(-bins // 16) * 16
    weight = jnp.pad(head_weight, ((0, bins_up - bins), (0, 0)))
    bias = jnp.pad(head_bias, (0, bins_up - bins), constant_values=-jnp.inf)[:, None]
    delta, first, second = call(
        head_kernel,
        "head",
        (rows(size), packs, packs),
        [
            ((width * channels // 2, width), F32), ((size * channels, width), F32),
            ((size, width), jnp.int32),
        ],
        24, 4 * macs, place, *got_inner, *got_edge, hidden_inner, hidden_edge,
        slope_two_inner, slope_two_edge, target, weight, weight.T, bias,
    )
    right, left = shifted(first, "row", -1), shifted(second, "row", 1)
    top, bottom = strips(delta, right, left)
    w1, w2 = back(first_block_kernel), back(second_block_kernel)
    kept_two, kept_one, inner_rows = call(
        backward_inner_kernel,
        "backward_inner",
        (sides(2 * d2), sides(d1), rows(inner, width, F32)),
        [
            ((size,) + ring, BF16), ((size - 2 * d2,) + ring, BF16),
            ((size + 2 * d2,) + ring, F32),
        ],
        32, 8 * macs, delta, right, left, slope_one_inner, w2, w1,
    )
    out = call(
        backward_edge_kernel,
        "backward_edge",
        jax.ShapeDtypeStruct((channels * size, width), F32),
        edge_rings,
        32, 4 * macs, top, bottom, kept_two, kept_one, inner_rows,
        slope_one_inner, slope_one_edge, w2, w1,
    )
    return out.reshape(channels, size, width)


def solution(mesh):
    in_specs = (P(None, "col", "row"), P(), P(), P(), P(), P(), P(), P("col", "row"))
    out_specs = P(None, "col", "row")
    return jax.shard_map(local, mesh=mesh, in_specs=in_specs, out_specs=out_specs, check_vma=False)
```

time: 152 us -> 122 us (0.80)
  waiting for transfers between devices: 66.3 us -> 41.4 us
  Pallas kernels: 48 us -> 29.1 us
  starting transfers between devices: 27.3 us -> 34 us
  local copies, waits for them, and re-layouts: 9.34 us -> 14.8 us
    pallas_call x4 -> x6, Pallas kernels: 48 us -> 29.1 us  [call(): pl.pallas_call(kernel, out_shape=outs, in_specs=places, out_specs=jax.tre...]
    ppermute x8, waiting for transfers between devices: 20.9 us -> 7 us  [shifted(): return lax.ppermute(tensor, axis, pairs)]
    ppermute x2 -> x4, waiting for transfers between devices: 45.4 us -> 34.4 us  [the longest x2 26 us: local(): lax.ppermute(sent_inner[k], ('row', 'col'), mirror_pairs(k))]
    ppermute x2 -> x4, starting transfers between devices: 5.15 us -> 12.5 us  [the longest x2 7.88 us: local(): lax.ppermute(sent_edge[k], ('row', 'col'), mirror_pairs(k))]
    transpose x4, local copies, waits for them, and re-layouts: 0.35 us -> 4.82 us  [back(): kernel[::-1, ::-1].transpose(0, 3, 1, 2).reshape(3 * channels, 3 * channels)]
    reshape x2, local copies, waits for them, and re-layouts: 0.33 us -> 2.18 us  [back(): kernel[::-1, ::-1].transpose(0, 3, 1, 2).reshape(3 * channels, 3 * channels)]
    unnamed x32 -> x26, local copies, waits for them, and re-layouts: 6.53 us -> 6.17 us
  transfers between devices with their start and end apart: 10 -> 12, of which waited for: 8 -> 6; matrix products, arithmetic and copies ran while one was open for 1% -> 8% of each run, Pallas kernels for 0% -> 14%
where the time goes in v1:
time: 122 us; the launch traced here: 121 us
  waiting for transfers between devices  41.4 us (34%)
  starting transfers between devices  34 us (28%)
  Pallas kernels  29.1 us (24%)
  local copies, waits for them, and re-layouts  14.8 us (12%)
  other arithmetic  1.63 us (1%)
    pallas_call x6, Pallas kernels, call(): pl.pallas_call(kernel, out_shape=outs, in_specs=places, out_specs=jax.tre...  29.1 us
    ppermute x2, waiting for transfers between devices, local(): lax.ppermute(sent_inner[k], ('row', 'col'), mirror_pairs(k))  26 us
    ppermute x8, starting transfers between devices, shifted(): return lax.ppermute(tensor, axis, pairs)  21.5 us
    ppermute x2, waiting for transfers between devices, local(): lax.ppermute(sent_edge[k], ('row', 'col'), mirror_pairs(k))  8.43 us
    ppermute x2, starting transfers between devices, local(): lax.ppermute(sent_edge[k], ('row', 'col'), mirror_pairs(k))  7.88 us
    ppermute x8, waiting for transfers between devices, shifted(): return lax.ppermute(tensor, axis, pairs)  7 us
    unnamed x26, local copies, waits for them, and re-layouts  6.17 us
    transpose x4, local copies, waits for them, and re-layouts, back(): kernel[::-1, ::-1].transpose(0, 3, 1, 2).reshape(3 * channels, 3 * channels)  4.82 us
  transfers between devices with their start and end apart: 12, of which 6 were waited for; matrix products, arithmetic and copies ran while one was open for 8% of the time, Pallas kernels for 14%

profile of v1, /device:TPU:6, one launch (start us, length us, event | category | flops | bytes accessed | tf_op | source)
XLA Modules:
  0.0 121.3 jit_solution(5097277647170418462)
XLA Ops:
  0.0 1.2 %copy-done.2 = bf16[64,64,128]{2,1,0:T(8,128)(2,1)S(1)} copy-done((bf16[64,64,128]{2,1,0:T(8,128)(2,1)S(1)}, bf16[64,64,128]{2,1,0:T(8,128)(2,1)}, u32[]{:S(2)}) %copy-start.2) | copy-done | bytes 1048600
  1.3 1.3 %prepare.1 = (bf16[64,64,128]{2,1,0:T(8,128)(2,1)S(1)}, bf16[8,64,128]{2,1,0:T(8,128)(2,1)S(1)}, bf16[8,64,128]{2,1,0:T(8,128)(2,1)S(1)}) custom-call(bf16[64,64,128]{2,1,0:T(8,128)(2,1)S(1)} %copy-done.2), custom_call_target="tpu_custom_call" | custom-call | flops 1 | bytes 8388608 | tf_op jit(solution)/shard_map/prepare/pallas_call | solution.py:500
  2.5 1.9 %collective-permute-start = (bf16[8,64,128]{2,1,0:T(8,128)(2,1)S(1)}, bf16[8,64,128]{2,1,0:T(8,128)(2,1)S(1)}, u32[]{:S(2)}, u32[]{:S(2)}) collective-permute-start(bf16[8,64,128]{2,1,0:T(8,128)(2,1)S(1)} %get-tuple-element.27), channel_id=1, source_target_pairs={{8,0},{16,8},{24,16},{9,1},{17,9},{25,17},{10,2},{18,10},{26,18},{... | collective-permute-start | bytes 393224 | tf_op jit(solution)/shard_map/ppermute | solution.py:443
  4.5 2.4 %collective-permute-start.1 = (bf16[8,64,128]{2,1,0:T(8,128)(2,1)S(1)}, bf16[8,64,128]{2,1,0:T(8,128)(2,1)S(1)}, u32[]{:S(2)}, u32[]{:S(2)}) collective-permute-start(bf16[8,64,128]{2,1,0:T(8,128)(2,1)S(1)} %get-tuple-element.28), channel_id=1, source_target_pairs={{0,8},{8,16},{16,24},{1,9},{9,17},{17,25},{2,10},{10,18},{18,26},{... | collective-permute-start | bytes 393224 | tf_op jit(solution)/shard_map/ppermute | solution.py:443
  7.6 3.2 %collective-permute-done.1.left_ref = bf16[8,64,128]{2,1,0:T(8,128)(2,1)S(1)} collective-permute-done((bf16[8,64,128]{2,1,0:T(8,128)(2,1)S(1)}, bf16[8,64,128]{2,1,0:T(8,128)(2,1)S(1)}, u32[]{:S(2)}, u32[]{:S(2)}) %collective-permute-start.1) | collective-permute-done | bytes 131104 | tf_op jit(solution)/shard_map/ppermute | solution.py:443
  10.8 3.5 %collective-permute-start.4 = (bf16[16,64,128]{2,1,0:T(8,128)(2,1)S(1)}, bf16[16,64,128]{2,1,0:T(8,128)(2,1)S(1)}, u32[]{:S(2)}, u32[]{:S(2)}) collective-permute-start(bf16[16,64,128]{2,1,0:T(8,128)(2,1)S(1)} %pad_maximum_fusion), channel_id=1, source_target_pairs={{0,1},{1,2},{2,3},{3,4},{4,5},{5,6},{6,7},{8,9},{9,10},{10,11},{11... | collective-permute-start | bytes 786440 | tf_op jit(solution)/shard_map/ppermute | solution.py:443
  14.3 2.4 %collective-permute-start.5 = (bf16[16,64,128]{2,1,0:T(8,128)(2,1)S(1)}, bf16[16,64,128]{2,1,0:T(8,128)(2,1)S(1)}, u32[]{:S(2)}, u32[]{:S(2)}) collective-permute-start(bf16[16,64,128]{2,1,0:T(8,128)(2,1)S(1)} %pad_maximum_fusion.1), channel_id=1, source_target_pairs={{1,0},{2,1},{3,2},{4,3},{5,4},{6,5},{7,6},{9,8},{10,9},{11,10},{12... | collective-permute-start | bytes 786440 | tf_op jit(solution)/shard_map/ppermute | solution.py:443
  17.9 8.0 %forward_inner.1 = (f32[2,8,64,256]{3,2,1,0:T(8,128)S(1)}, f32[2,8,64,256]{3,2,1,0:T(8,128)S(1)}, bf16[40,64,128]{2,1,0:T(8,128)(2,1)S(1)}, f32[56,64,256]{2,1,0...) custom-call(s32[4]{0:T(128)S(1)} %pad_add_fusion.place_ref, ...), custom_call_target="tpu_custom_call" | custom-call | flops 2415919104 | bytes 8388608 | tf_op jit(solution)/shard_map/forward_inner/pallas_call | solution.py:500
  26.0 1.8 %copy-done = f32[56,64,256]{2,1,0:T(8,128)} copy-done((f32[56,64,256]{2,1,0:T(8,128)}, f32[56,64,256]{2,1,0:T(8,128)S(1)}, u32[]{:S(2)}) %copy-start) | copy-done | bytes 3670040
  27.7 1.9 %collective-permute-start.2 = (bf16[41,32,128]{2,1,0:T(8,128)(2,1)S(1)}, bf16[41,32,128]{2,1,0:T(8,128)(2,1)S(1)}, u32[]{:S(2)}, u32[]{:S(2)}) collective-permute-start(bf16[41,32,128]{2,1,0:T(8,128)(2,1)S(1)} %get-tuple-element.29), channel_id=1, source_target_pairs={{0,0},{8,2},{16,4},{24,6},{1,1},{9,3},{17,5},{25,7},{2,8},{10,10},... | collective-permute-start | bytes 1007624 | tf_op jit(solution)/shard_map/ppermute | solution.py:538
  29.7 2.7 %collective-permute-start.3 = (bf16[41,32,128]{2,1,0:T(8,128)(2,1)S(1)}, bf16[41,32,128]{2,1,0:T(8,128)(2,1)S(1)}, u32[]{:S(2)}, u32[]{:S(2)}) collective-permute-start(bf16[41,32,128]{2,1,0:T(8,128)(2,1)S(1)} %get-tuple-element.30), channel_id=1, source_target_pairs={{0,1},{8,3},{16,5},{24,7},{1,0},{9,2},{17,4},{25,6},{2,9},{10,11},... | collective-permute-start | bytes 1007624 | tf_op jit(solution)/shard_map/ppermute | solution.py:538
  32.4 2.8 %forward_edge.1 = (bf16[24,64,128]{2,1,0:T(8,128)(2,1)S(1)}, f32[2,12,64,256]{3,2,1,0:T(8,128)S(1)}, f32[24,64,128]{2,1,0:T(8,128)S(1)}, bf16[24,32,128]{2,1,0:T(8,128)(2,1)S(1)}, bf16[24,32,128]{2,1,0:T(8,128)(2,1)S(1)}) custom-call(s32[4]{0:T(128)S(1)} %pad_add_fusion.place_ref, bf16[16,64,128]{2,1,0:T(8,128)(2,1)S(1)} %collective-permute-done.4.top_ref, ...), custom_call_target="tpu_custom_call" | custom-call | flops 1207959552 | bytes 8388608 | tf_op jit(solution)/shard_map/forward_edge/pallas_call | solution.py:500
  35.2 3.6 %collective-permute-start.6 = (bf16[24,32,128]{2,1,0:T(8,128)(2,1)S(1)}, bf16[24,32,128]{2,1,0:T(8,128)(2,1)S(1)}, u32[]{:S(2)}, u32[]{:S(2)}) collective-permute-start(bf16[24,32,128]{2,1,0:T(8,128)(2,1)S(1)} %get-tuple-element.33), channel_id=1, source_target_pairs={{0,0},{8,2},{16,4},{24,6},{1,1},{9,3},{17,5},{25,7},{2,8},{10,10},... | collective-permute-start | bytes 589832 | tf_op jit(solution)/shard_map/ppermute | solution.py:549
  38.8 4.3 %collective-permute-start.7 = (bf16[24,32,128]{2,1,0:T(8,128)(2,1)S(1)}, bf16[24,32,128]{2,1,0:T(8,128)(2,1)S(1)}, u32[]{:S(2)}, u32[]{:S(2)}) collective-permute-start(bf16[24,32,128]{2,1,0:T(8,128)(2,1)S(1)} %get-tuple-element.34), channel_id=1, source_target_pairs={{0,1},{8,3},{16,5},{24,7},{1,0},{9,2},{17,4},{25,6},{2,9},{10,11},... | collective-permute-start | bytes 589832 | tf_op jit(solution)/shard_map/ppermute | solution.py:549
  43.8 18.7 %collective-permute-done.2.inner_a_ref = bf16[41,32,128]{2,1,0:T(8,128)(2,1)S(1)} collective-permute-done((bf16[41,32,128]{2,1,0:T(8,128)(2,1)S(1)}, bf16[41,32,128]{2,1,0:T(8,128)(2,1)S(1)}, u32[]{:S(2)}, u32[]{:S(2)}) %collective-permute-start.2) | collective-permute-done | bytes 335904 | tf_op jit(solution)/shard_map/ppermute | solution.py:538
  62.4 7.3 %collective-permute-done.3.inner_b_ref = bf16[41,32,128]{2,1,0:T(8,128)(2,1)S(1)} collective-permute-done((bf16[41,32,128]{2,1,0:T(8,128)(2,1)S(1)}, bf16[41,32,128]{2,1,0:T(8,128)(2,1)S(1)}, u32[]{:S(2)}, u32[]{:S(2)}) %collective-permute-start.3) | collective-permute-done | bytes 335904 | tf_op jit(solution)/shard_map/ppermute | solution.py:538
  69.8 4.1 %collective-permute-done.6.edge_a_ref = bf16[24,32,128]{2,1,0:T(8,128)(2,1)S(1)} collective-permute-done((bf16[24,32,128]{2,1,0:T(8,128)(2,1)S(1)}, bf16[24,32,128]{2,1,0:T(8,128)(2,1)S(1)}, u32[]{:S(2)}, u32[]{:S(2)}) %collective-permute-start.6) | collective-permute-done | bytes 196640 | tf_op jit(solution)/shard_map/ppermute | solution.py:549
  73.9 4.4 %collective-permute-done.7.edge_b_ref = bf16[24,32,128]{2,1,0:T(8,128)(2,1)S(1)} collective-permute-done((bf16[24,32,128]{2,1,0:T(8,128)(2,1)S(1)}, bf16[24,32,128]{2,1,0:T(8,128)(2,1)S(1)}, u32[]{:S(2)}, u32[]{:S(2)}) %collective-permute-start.7) | collective-permute-done | bytes 196640 | tf_op jit(solution)/shard_map/ppermute | solution.py:549
  78.2 6.6 %head.1 = (bf16[64,64,128]{2,1,0:T(8,128)(2,1)S(1)}, bf16[8,64,128]{2,1,0:T(8,128)(2,1)S(1)}, bf16[8,64,128]{2,1,0:T(8,128)(2,1)S(1)}) custom-call(s32[4]{0:T(128)S(1)} %pad_add_fusion.place_ref, bf16[41,32,128]{2,1,0:T(8,128)(2,1)S(1)} %collective-permute-done.2.inner_a_ref, bf16[41,32,128]{2,1,0:T(8,128)(2,1)S(1)} %collective-permute-done.3.inner_b_ref, ...), custom_call_target="tpu_custom_call" | custom-call | flops 1207959552 | bytes 8388608 | tf_op jit(solution)/shard_map/head/pallas_call | solution.py:500
  84.8 2.1 %collective-permute-start.8 = (bf16[8,64,128]{2,1,0:T(8,128)(2,1)S(1)}, bf16[8,64,128]{2,1,0:T(8,128)(2,1)S(1)}, u32[]{:S(2)}, u32[]{:S(2)}) collective-permute-start(bf16[8,64,128]{2,1,0:T(8,128)(2,1)S(1)} %get-tuple-element.40), channel_id=1, source_target_pairs={{8,0},{16,8},{24,16},{9,1},{17,9},{25,17},{10,2},{18,10},{26,18},{... | collective-permute-start | bytes 393224 | tf_op jit(solution)/shard_map/ppermute | solution.py:443
  86.9 2.4 %collective-permute-start.9 = (bf16[8,64,128]{2,1,0:T(8,128)(2,1)S(1)}, bf16[8,64,128]{2,1,0:T(8,128)(2,1)S(1)}, u32[]{:S(2)}, u32[]{:S(2)}) collective-permute-start(bf16[8,64,128]{2,1,0:T(8,128)(2,1)S(1)} %get-tuple-element.41), channel_id=1, source_target_pairs={{0,8},{8,16},{16,24},{1,9},{9,17},{17,25},{2,10},{10,18},{18,26},{... | collective-permute-start | bytes 393224 | tf_op jit(solution)/shard_map/ppermute | solution.py:443
  89.4 3.8 %collective-permute-done.9.left_ref = bf16[8,64,128]{2,1,0:T(8,128)(2,1)S(1)} collective-permute-done((bf16[8,64,128]{2,1,0:T(8,128)(2,1)S(1)}, bf16[8,64,128]{2,1,0:T(8,128)(2,1)S(1)}, u32[]{:S(2)}, u32[]{:S(2)}) %collective-permute-start.9) | collective-permute-done | bytes 131104 | tf_op jit(solution)/shard_map/ppermute | solution.py:443
  93.9 3.2 %collective-permute-start.11 = (bf16[16,64,128]{2,1,0:T(8,128)(2,1)}, bf16[16,64,128]{2,1,0:T(8,128)(2,1)S(1)}, u32[]{:S(2)}, u32[]{:S(2)}) collective-permute-start(bf16[16,64,128]{2,1,0:T(8,128)(2,1)} %pad_maximum_fusion.3), channel_id=1, source_target_pairs={{1,0},{2,1},{3,2},{4,3},{5,4},{6,5},{7,6},{9,8},{10,9},{11,10},{12... | collective-permute-start | bytes 786440 | tf_op jit(solution)/shard_map/ppermute | solution.py:443
  97.9 3.7 %collective-permute-start.10 = (bf16[16,64,128]{2,1,0:T(8,128)(2,1)}, bf16[16,64,128]{2,1,0:T(8,128)(2,1)S(1)}, u32[]{:S(2)}, u32[]{:S(2)}) collective-permute-start(bf16[16,64,128]{2,1,0:T(8,128)(2,1)} %pad_maximum_fusion.2), channel_id=1, source_target_pairs={{0,1},{1,2},{2,3},{3,4},{4,5},{5,6},{6,7},{8,9},{9,10},{10,11},{11... | collective-permute-start | bytes 786440 | tf_op jit(solution)/shard_map/ppermute | solution.py:443
  102.3 1.7 %copy.29 = bf16[3,64,3,64]{3,2,1,0:T(4,128)(2,1)} copy(bf16[3,64,3,64]{1,3,2,0:T(8,128)(2,1)} %reverse_bitcast_fusion.1) | data formatting | bytes 147456 | tf_op jit(solution)/shard_map/transpose | solution.py:487
  104.0 1.1 reshape.17.w2_ref
  105.1 1.7 %copy.30 = bf16[3,64,3,64]{3,2,1,0:T(4,128)(2,1)} copy(bf16[3,64,3,64]{1,3,2,0:T(8,128)(2,1)} %reverse_bitcast_fusion) | data formatting | bytes 147456 | tf_op jit(solution)/shard_map/transpose | solution.py:487
  106.8 1.1 reshape.18.w1_ref
  107.9 2.0 %copy-done.1 = f32[56,64,256]{2,1,0:T(8,128)S(1)} copy-done((f32[56,64,256]{2,1,0:T(8,128)S(1)}, f32[56,64,256]{2,1,0:T(8,128)}, u32[]{:S(2)}) %copy-start.1) | copy-done | bytes 3670040
  110.0 0.9 copy-done.4
  110.9 6.0 %backward_inner.1 = (f32[2,16,64,256]{3,2,1,0:T(8,128)S(1)}, f32[2,4,64,256]{3,2,1,0:T(8,128)S(1)}, f32[40,64,128]{2,1,0:T(8,128)S(1)}) custom-call(bf16[64,64,128]{2,1,0:T(8,128)(2,1)S(1)} %get-tuple-element.39.main_ref, bf16[8,64,128]{2,1,0:T(8,128)(2,1)S(1)} %collective-permute-done.8.right_ref, bf16[8,64,128]{2,1,0:T(8,128)(2,1)S(1)} %copy-done.4, ...), custom_call_target="tpu_custom_call" | custom-call | flops 2415919104 | bytes 8388608 | tf_op jit(solution)/shard_map/backward_inner/pallas_call | solution.py:500
  116.9 4.4 %backward_edge.1 = f32[4096,128]{1,0:T(8,128)} custom-call(bf16[16,64,128]{2,1,0:T(8,128)(2,1)S(1)} %collective-permute-done.10.top_ref, bf16[16,64,128]{2,1,0:T(8,128)(2,1)S(1)} %collective-permute-done.11.bottom_ref, f32[2,16,64,256]{3,2,1,0:T(8,128)S(1)} %get-tuple-element.43.kept_two_ref, f32[2,4,64,256]{3,2,1,0:T(8,128)S(1)} %get-tuple-element.44.kept_one_ref, ...), custom_call_target="tpu_custom_call" | custom-call | flops 1207959552 | bytes 8388608 | tf_op jit(solution)/shard_map/backward_edge/pallas_call | solution.py:500
  (51 shorter events, 4.9 us)
Async XLA Ops:
  0.0 1.2 %copy-start.2 = (bf16[64,64,128]{2,1,0:T(8,128)(2,1)S(1)}, bf16[64,64,128]{2,1,0:T(8,128)(2,1)}, u32[]{:S(2)}) copy-start(bf16[64,64,128]{2,1,0:T(8,128)(2,1)} %x_ref.1) | copy-start | bytes 3145732
  1.2 15.6 %copy-start.7 = (bf16[3,3,64,64]{3,2,1,0:T(8,128)(2,1)S(1)}, bf16[3,3,64,64]{3,2,1,0:T(8,128)(2,1)}, u32[]{:S(2)}) copy-start(bf16[3,3,64,64]{3,2,1,0:T(8,128)(2,1)} %param.9) | copy-start | bytes 221188
  1.2 15.9 %copy-start.6 = (bf16[3,3,64,64]{3,2,1,0:T(8,128)(2,1)S(1)}, bf16[3,3,64,64]{3,2,1,0:T(8,128)(2,1)}, u32[]{:S(2)}) copy-start(bf16[3,3,64,64]{3,2,1,0:T(8,128)(2,1)} %param.11) | copy-start | bytes 221188
  1.2 16.2 %copy-start.10 = (f32[64]{0:T(128)S(1)}, f32[64]{0:T(128)}, u32[]{:S(2)}) copy-start(f32[64]{0:T(128)} %param.10) | copy-start | bytes 772
  1.2 16.3 %copy-start.11 = (f32[64]{0:T(128)S(1)}, f32[64]{0:T(128)}, u32[]{:S(2)}) copy-start(f32[64]{0:T(128)} %param.12) | copy-start | bytes 772
  1.2 16.4 %copy-start.9 = (bf16[37,64]{1,0:T(8,128)(2,1)S(1)}, bf16[37,64]{1,0:T(8,128)(2,1)}, u32[]{:S(2)}) copy-start(bf16[37,64]{1,0:T(8,128)(2,1)} %param.13) | copy-start | bytes 14212
  1.2 16.7 %copy-start.5 = (s32[64,128]{1,0:T(8,128)S(1)}, s32[64,128]{1,0:T(8,128)}, u32[]{:S(2)}) copy-start(s32[64,128]{1,0:T(8,128)} %target_ref.3) | copy-start | bytes 98308
  2.5 5.1 %collective-permute-start = (bf16[8,64,128]{2,1,0:T(8,128)(2,1)S(1)}, bf16[8,64,128]{2,1,0:T(8,128)(2,1)S(1)}, u32[]{:S(2)}, u32[]{:S(2)}) collective-permute-start(bf16[8,64,128]{2,1,0:T(8,128)(2,1)S(1)} %get-tuple-element.27), channel_id=1, source_target_pairs={{8,0},{16,8},{24,16},{9,1},{17,9},{25,17},{10,2},{18,10},{26,18},{... | collective-permute-start | bytes 393224 | tf_op jit(solution)/shard_map/ppermute | solution.py:443
  4.5 6.3 %collective-permute-start.1 = (bf16[8,64,128]{2,1,0:T(8,128)(2,1)S(1)}, bf16[8,64,128]{2,1,0:T(8,128)(2,1)S(1)}, u32[]{:S(2)}, u32[]{:S(2)}) collective-permute-start(bf16[8,64,128]{2,1,0:T(8,128)(2,1)S(1)} %get-tuple-element.28), channel_id=1, source_target_pairs={{0,8},{8,16},{16,24},{1,9},{9,17},{17,25},{2,10},{10,18},{18,26},{... | collective-permute-start | bytes 393224 | tf_op jit(solution)/shard_map/ppermute | solution.py:443
  10.8 21.6 %collective-permute-start.4 = (bf16[16,64,128]{2,1,0:T(8,128)(2,1)S(1)}, bf16[16,64,128]{2,1,0:T(8,128)(2,1)S(1)}, u32[]{:S(2)}, u32[]{:S(2)}) collective-permute-start(bf16[16,64,128]{2,1,0:T(8,128)(2,1)S(1)} %pad_maximum_fusion), channel_id=1, source_target_pairs={{0,1},{1,2},{2,3},{3,4},{4,5},{5,6},{6,7},{8,9},{9,10},{10,11},{11... | collective-permute-start | bytes 786440 | tf_op jit(solution)/shard_map/ppermute | solution.py:443
  14.3 18.1 %collective-permute-start.5 = (bf16[16,64,128]{2,1,0:T(8,128)(2,1)S(1)}, bf16[16,64,128]{2,1,0:T(8,128)(2,1)S(1)}, u32[]{:S(2)}, u32[]{:S(2)}) collective-permute-start(bf16[16,64,128]{2,1,0:T(8,128)(2,1)S(1)} %pad_maximum_fusion.1), channel_id=1, source_target_pairs={{1,0},{2,1},{3,2},{4,3},{5,4},{6,5},{7,6},{9,8},{10,9},{11,10},{12... | collective-permute-start | bytes 786440 | tf_op jit(solution)/shard_map/ppermute | solution.py:443
  26.0 1.8 %copy-start = (f32[56,64,256]{2,1,0:T(8,128)}, f32[56,64,256]{2,1,0:T(8,128)S(1)}, u32[]{:S(2)}) copy-start(f32[56,64,256]{2,1,0:T(8,128)S(1)} %get-tuple-element.42.slope_one_ref.slope_inner_ref) | copy-start | bytes 11010052
  27.7 34.7 %collective-permute-start.2 = (bf16[41,32,128]{2,1,0:T(8,128)(2,1)S(1)}, bf16[41,32,128]{2,1,0:T(8,128)(2,1)S(1)}, u32[]{:S(2)}, u32[]{:S(2)}) collective-permute-start(bf16[41,32,128]{2,1,0:T(8,128)(2,1)S(1)} %get-tuple-element.29), channel_id=1, source_target_pairs={{0,0},{8,2},{16,4},{24,6},{1,1},{9,3},{17,5},{25,7},{2,8},{10,10},... | collective-permute-start | bytes 1007624 | tf_op jit(solution)/shard_map/ppermute | solution.py:538
  29.7 40.1 %collective-permute-start.3 = (bf16[41,32,128]{2,1,0:T(8,128)(2,1)S(1)}, bf16[41,32,128]{2,1,0:T(8,128)(2,1)S(1)}, u32[]{:S(2)}, u32[]{:S(2)}) collective-permute-start(bf16[41,32,128]{2,1,0:T(8,128)(2,1)S(1)} %get-tuple-element.30), channel_id=1, source_target_pairs={{0,1},{8,3},{16,5},{24,7},{1,0},{9,2},{17,4},{25,6},{2,9},{10,11},... | collective-permute-start | bytes 1007624 | tf_op jit(solution)/shard_map/ppermute | solution.py:538
  35.2 38.6 %collective-permute-start.6 = (bf16[24,32,128]{2,1,0:T(8,128)(2,1)S(1)}, bf16[24,32,128]{2,1,0:T(8,128)(2,1)S(1)}, u32[]{:S(2)}, u32[]{:S(2)}) collective-permute-start(bf16[24,32,128]{2,1,0:T(8,128)(2,1)S(1)} %get-tuple-element.33), channel_id=1, source_target_pairs={{0,0},{8,2},{16,4},{24,6},{1,1},{9,3},{17,5},{25,7},{2,8},{10,10},... | collective-permute-start | bytes 589832 | tf_op jit(solution)/shard_map/ppermute | solution.py:549
  38.8 39.4 %collective-permute-start.7 = (bf16[24,32,128]{2,1,0:T(8,128)(2,1)S(1)}, bf16[24,32,128]{2,1,0:T(8,128)(2,1)S(1)}, u32[]{:S(2)}, u32[]{:S(2)}) collective-permute-start(bf16[24,32,128]{2,1,0:T(8,128)(2,1)S(1)} %get-tuple-element.34), channel_id=1, source_target_pairs={{0,1},{8,3},{16,5},{24,7},{1,0},{9,2},{17,4},{25,6},{2,9},{10,11},... | collective-permute-start | bytes 589832 | tf_op jit(solution)/shard_map/ppermute | solution.py:549
  84.8 16.8 %copy-start.8 = (bf16[3,3,64,64]{3,2,1,0:T(8,128)(2,1)S(1)}, bf16[3,3,64,64]{3,2,1,0:T(8,128)(2,1)}, u32[]{:S(2)}) copy-start(bf16[3,3,64,64]{3,2,1,0:T(8,128)(2,1)} %param.9) | copy-start | bytes 221188
  84.8 4.6 %collective-permute-start.8 = (bf16[8,64,128]{2,1,0:T(8,128)(2,1)S(1)}, bf16[8,64,128]{2,1,0:T(8,128)(2,1)S(1)}, u32[]{:S(2)}, u32[]{:S(2)}) collective-permute-start(bf16[8,64,128]{2,1,0:T(8,128)(2,1)S(1)} %get-tuple-element.40), channel_id=1, source_target_pairs={{8,0},{16,8},{24,16},{9,1},{17,9},{25,17},{10,2},{18,10},{26,18},{... | collective-permute-start | bytes 393224 | tf_op jit(solution)/shard_map/ppermute | solution.py:443
  86.9 6.3 %collective-permute-start.9 = (bf16[8,64,128]{2,1,0:T(8,128)(2,1)S(1)}, bf16[8,64,128]{2,1,0:T(8,128)(2,1)S(1)}, u32[]{:S(2)}, u32[]{:S(2)}) collective-permute-start(bf16[8,64,128]{2,1,0:T(8,128)(2,1)S(1)} %get-tuple-element.41), channel_id=1, source_target_pairs={{0,8},{8,16},{16,24},{1,9},{9,17},{17,25},{2,10},{10,18},{18,26},{... | collective-permute-start | bytes 393224 | tf_op jit(solution)/shard_map/ppermute | solution.py:443
  93.2 9.1 %copy-start.3 = (bf16[8,64,128]{2,1,0:T(8,128)(2,1)}, bf16[8,64,128]{2,1,0:T(8,128)(2,1)S(1)}, u32[]{:S(2)}) copy-start(bf16[8,64,128]{2,1,0:T(8,128)(2,1)S(1)} %collective-permute-done.9.left_ref) | copy-start | bytes 393220
  93.9 23.0 %collective-permute-start.11 = (bf16[16,64,128]{2,1,0:T(8,128)(2,1)}, bf16[16,64,128]{2,1,0:T(8,128)(2,1)S(1)}, u32[]{:S(2)}, u32[]{:S(2)}) collective-permute-start(bf16[16,64,128]{2,1,0:T(8,128)(2,1)} %pad_maximum_fusion.3), channel_id=1, source_target_pairs={{1,0},{2,1},{3,2},{4,3},{5,4},{6,5},{7,6},{9,8},{10,9},{11,10},{12... | collective-permute-start | bytes 786440 | tf_op jit(solution)/shard_map/ppermute | solution.py:443
  97.9 19.1 %collective-permute-start.10 = (bf16[16,64,128]{2,1,0:T(8,128)(2,1)}, bf16[16,64,128]{2,1,0:T(8,128)(2,1)S(1)}, u32[]{:S(2)}, u32[]{:S(2)}) collective-permute-start(bf16[16,64,128]{2,1,0:T(8,128)(2,1)} %pad_maximum_fusion.2), channel_id=1, source_target_pairs={{0,1},{1,2},{2,3},{3,4},{4,5},{5,6},{6,7},{8,9},{9,10},{10,11},{11... | collective-permute-start | bytes 786440 | tf_op jit(solution)/shard_map/ppermute | solution.py:443
  107.9 2.0 %copy-start.1 = (f32[56,64,256]{2,1,0:T(8,128)S(1)}, f32[56,64,256]{2,1,0:T(8,128)}, u32[]{:S(2)}) copy-start(f32[56,64,256]{2,1,0:T(8,128)} %copy-done) | copy-start | bytes 11010052
  110.0 0.9 copy-start.4

commit v2 on v1

--- a/solution.py
+++ b/solution.py
@@ -12,7 +12,6 @@
 F32 = jnp.float32
 BF16 = jnp.bfloat16
 VMEM = pl.BlockSpec(memory_space=pltpu.VMEM)
-SMEM = pl.BlockSpec(memory_space=pltpu.SMEM)
 
 
 def params(megabytes):
@@ -167,10 +166,10 @@
     return jnp.where(up, pre, decay - 1.0), jnp.where(up, 1.0, decay)
 
 
-def lanes_inside(place_ref, width):
+def lanes_inside(width):
     lane = lanes_of((1, 2 * width))
-    q = jnp.where(lane < width + width // 2, lane, lane - 2 * width) + place_ref[1] * width
-    return jnp.where((q >= 0) & (q < place_ref[3] * width), 1.0, 0.0)
+    q = jnp.where(lane < width + width // 2, lane, lane - 2 * width) + lax.axis_index("row") * width
+    return jnp.where((q >= 0) & (q < lax.axis_size("row") * width), 1.0, 0.0)
 
 
 def put_piece(send_refs, mine, p, hidden):
@@ -196,18 +195,64 @@
         pack_edges([turned[i] for i in range(per)], first_ref, second_ref, block)
 
 
+def weights_kernel(
+    k1_ref, k2_ref, b1_ref, b2_ref, head_ref, head_bias_ref,
+    ahead_1_ref, ahead_2_ref, back_1_ref, back_2_ref,
+    column_1_ref, column_2_ref, head_up_ref, head_t_ref, head_column_ref,
+    scratch_ref,
+):
+    for kernel_ref, ahead_ref, back_ref in (
+        (k1_ref, ahead_1_ref, back_1_ref), (k2_ref, ahead_2_ref, back_2_ref)
+    ):
+        taps = [[kernel_ref[t, s].astype(F32) for s in range(3)] for t in range(3)]
+        ahead = [jnp.concatenate(taps[t], axis=1) for t in range(3)]
+        ahead_ref[...] = jnp.concatenate(ahead, axis=0).astype(BF16)
+        back = [
+            jnp.concatenate([taps[2 - t][2 - s].T for s in range(3)], axis=1) for t in range(3)
+        ]
+        back_ref[...] = jnp.concatenate(back, axis=0).astype(BF16)
+
+    def column(row_ref):
+        row = row_ref[...]
+        return jnp.broadcast_to(row, (column_1_ref.shape[1], row.shape[1])).T
+
+    column_1_ref[...] = column(b1_ref)
+    column_2_ref[...] = column(b2_ref)
+    bins = head_ref.shape[0]
+    head_column_ref[...] = jnp.full(head_column_ref.shape, -jnp.inf, F32)
+    head_column_ref[:bins] = column(head_bias_ref)
+    scratch_ref[...] = jnp.zeros(scratch_ref.shape, F32)
+    scratch_ref[:bins] = head_ref[...].astype(F32)
+    head_up_ref[...] = scratch_ref[...].astype(BF16)
+    head_t_ref[...] = scratch_ref[...].T.astype(BF16)
+
+
+def strips_kernel(main_ref, right_ref, left_ref, down_ref, up_ref):
+    size = main_ref.shape[0]
+    blocks = right_ref.shape[0]
+    near = (down_ref.shape[0] - MARGIN) // 2
+    for k in range(MARGIN):
+        down_ref[k] = main_ref[size - MARGIN + k]
+        up_ref[k] = main_ref[k]
+    for k in range(near):
+        down_ref[MARGIN + k] = right_ref[blocks - near + k]
+        down_ref[MARGIN + near + k] = left_ref[blocks - near + k]
+        up_ref[MARGIN + k] = right_ref[k]
+        up_ref[MARGIN + near + k] = left_ref[k]
+
+
 def forward_inner_kernel(
-    place_ref, main_ref, right_ref, left_ref, target_ref, w1_ref, b1_ref, w2_ref, b2_ref,
+    main_ref, right_ref, left_ref, target_ref, w1_ref, b1_ref, w2_ref, b2_ref,
     kept_one_ref, kept_two_ref, hidden_ref, slope_one_ref, slope_two_ref, send_a_ref, send_b_ref,
     ring_ref, near_ref, sums_ref,
 ):
     size, channels, width = main_ref.shape
     d1, d2 = DILATION_FIRST, DILATION_SECOND
     main_ring(main_ref, right_ref, left_ref, ring_ref)
-    lane_ok = lanes_inside(place_ref, width)
-    mine = lax.rem(place_ref[0], width // size)
-    b1 = b1_ref[...]
-    b2 = b2_ref[...]
+    lane_ok = lanes_inside(width)
+    mine = lax.rem(lax.axis_index("col"), width // size)
+    b1 = jnp.concatenate([b1_ref[...]] * 2, axis=1)
+    b2 = jnp.concatenate([b2_ref[...]] * 2, axis=1)
 
     def finish_one(i, total):
         hidden, slope = activated(total + b1)
@@ -232,17 +277,17 @@
 
 
 def forward_edge_kernel(
-    place_ref, top_ref, bottom_ref, kept_one_ref, kept_two_ref, w1_ref, b1_ref, w2_ref, b2_ref,
+    top_ref, bottom_ref, kept_one_ref, kept_two_ref, w1_ref, b1_ref, w2_ref, b2_ref,
     hidden_ref, slope_one_ref, slope_two_ref, send_a_ref, send_b_ref,
     ring_ref, near_ref, parts_ref,
 ):
     width = hidden_ref.shape[-1]
     size = width // 2
     d1, d2 = DILATION_FIRST, DILATION_SECOND
-    lane_ok = lanes_inside(place_ref, width)
-    mine = lax.rem(place_ref[0], width // size)
-    b1 = b1_ref[...]
-    b2 = b2_ref[...]
+    lane_ok = lanes_inside(width)
+    mine = lax.rem(lax.axis_index("col"), width // size)
+    b1 = jnp.concatenate([b1_ref[...]] * 2, axis=1)
+    b2 = jnp.concatenate([b2_ref[...]] * 2, axis=1)
     w1 = w1_ref[...]
     w2 = w2_ref[...]
     for below, strip_ref in enumerate((top_ref, bottom_ref)):
@@ -252,8 +297,8 @@
 
         def finish_one(i, total):
             hidden, slope = activated(total + b1)
-            p = (size - d1 if below else d1 - MARGIN) + i + place_ref[0] * size
-            ok = lane_ok * jnp.where((p >= 0) & (p < place_ref[2] * size), 1.0, 0.0)
+            p = (size - d1 if below else d1 - MARGIN) + i + lax.axis_index("col") * size
+            ok = lane_ok * jnp.where((p >= 0) & (p < lax.axis_size("col") * size), 1.0, 0.0)
             near[i] = (hidden * ok).astype(BF16)
             slope_one_ref[below, i] = slope * ok
 
@@ -276,7 +321,7 @@
 
 
 def head_kernel(
-    place_ref, inner_a_ref, inner_b_ref, edge_a_ref, edge_b_ref,
+    inner_a_ref, inner_b_ref, edge_a_ref, edge_b_ref,
     hidden_inner_ref, hidden_edge_ref, slope_inner_ref, slope_edge_ref, target_ref,
     weight_ref, weight_t_ref, bias_ref,
     delta_ref, first_ref, second_ref,
@@ -285,7 +330,7 @@
     size, channels, width = delta_ref.shape
     half = channels // 2
     group = width // size
-    mine = lax.rem(place_ref[0], group)
+    mine = lax.rem(lax.axis_index("col"), group)
     inner = size - 2 * MARGIN
 
     def widen(source_a_ref, source_b_ref, row, p):
@@ -318,7 +363,7 @@
     bins = weight_ref.shape[0]
     weight = weight_ref[...]
     weight_t = weight_t_ref[...]
-    bias = bias_ref[...]
+    bias = jnp.concatenate([bias_ref[...]] * 2, axis=1)
     bin_id = lax.broadcasted_iota(jnp.int32, (bins, 2 * width), 0)
     per = width // SLOT
 
@@ -443,13 +488,6 @@
     return lax.ppermute(tensor, axis, pairs)
 
 
-def strips(main, right, left):
-    near = -(-MARGIN // (main.shape[-1] // SLOT))
-    top = shifted(jnp.concatenate([main[-MARGIN:], right[-near:], left[-near:]]), "col", 1)
-    bottom = shifted(jnp.concatenate([main[:MARGIN], right[:near], left[:near]]), "col", -1)
-    return top, bottom
-
-
 def mirror_pairs(step):
     col_count, row_count = lax.axis_size("col"), lax.axis_size("row")
     group = col_count // row_count
@@ -473,19 +511,6 @@
     channels, size, width = pair_features.shape
     d1, d2 = DILATION_FIRST, DILATION_SECOND
     per = width // SLOT
-    place = jnp.stack(
-        [
-            lax.axis_index("col"), lax.axis_index("row"),
-            jnp.int32(lax.axis_size("col")), jnp.int32(lax.axis_size("row")),
-        ]
-    ).astype(jnp.int32)
-
-    def ahead(kernel):
-        return kernel.transpose(0, 2, 1, 3).reshape(3 * channels, 3 * channels)
-
-    def back(kernel):
-        return kernel[::-1, ::-1].transpose(0, 3, 1, 2).reshape(3 * channels, 3 * channels)
-
     def rows(count, lanes=width, kind=BF16):
         return jax.ShapeDtypeStruct((count, channels, lanes), kind)
 
@@ -496,11 +521,10 @@
         return jax.ShapeDtypeStruct((count, channels // 2, width), BF16)
 
     def call(kernel, name, outs, scratch, megabytes, flops, *operands):
-        places = [SMEM if operand is place else VMEM for operand in operands]
         return pl.pallas_call(
             kernel,
             out_shape=outs,
-            in_specs=places,
+            in_specs=[VMEM] * len(operands),
             out_specs=jax.tree.map(lambda _: VMEM, outs),
             scratch_shapes=[pltpu.VMEM(shape, kind) for shape, kind in scratch],
             compiler_params=params(megabytes),
@@ -515,13 +539,33 @@
     macs = 9 * channels * channels * size * width
 
     packs = rows(size // per)
+    square = jax.ShapeDtypeStruct((3 * channels, 3 * channels), BF16)
+    bins = head_weight.shape[0]
+    bins_up = -(-bins // 16) * 16
+    column = jax.ShapeDtypeStruct((channels, width), F32)
+    w1, w2, back_1, back_2, b1, b2, weight, weight_t, bias = call(
+        weights_kernel,
+        "weights",
+        (square,) * 4 + (
+            column, column, jax.ShapeDtypeStruct((bins_up, channels), BF16),
+            jax.ShapeDtypeStruct((channels, bins_up), BF16),
+            jax.ShapeDtypeStruct((bins_up, width), F32),
+        ),
+        [((bins_up, channels), F32)],
+        4, macs // 4, first_block_kernel, second_block_kernel, first_block_bias[None],
+        second_block_bias[None], head_weight, head_bias[None],
+    )
+
+    def strips(main, right, left):
+        strip = rows(MARGIN + 2 * -(-MARGIN // per))
+        down, up = call(strips_kernel, "strips", (strip, strip), [], 4, 1, main, right, left)
+        return shifted(down, "col", 1), shifted(up, "col", -1)
+
     main, first, second = call(
-        prepare_kernel, "prepare", (rows(size), packs, packs), [], 24, 1, pair_features
+        prepare_kernel, "prepare", (rows(size), packs, packs), [], 8, 1, pair_features
     )
     right, left = shifted(first, "row", -1), shifted(second, "row", 1)
     top, bottom = strips(main, right, left)
-    w1, w2 = ahead(first_block_kernel), ahead(second_block_kernel)
-    b1, b2 = first_block_bias[:, None], second_block_bias[:, None]
     kept_one, kept_two, hidden_inner, slope_one_inner, slope_two_inner, *sent_inner = call(
         forward_inner_kernel,
         "forward_inner",
@@ -533,7 +577,7 @@
             ((size,) + ring, BF16), ((size - 2 * d1,) + ring, BF16),
             ((size + 2 * d1,) + ring, F32),
         ],
-        32, 8 * macs, place, main, right, left, target, w1, b1, w2, b2,
+        18, 8 * macs, main, right, left, target, w1, b1, w2, b2,
     )
     got_inner = [lax.ppermute(sent_inner[k], ("row", "col"), mirror_pairs(k)) for k in range(2)]
     hidden_edge, slope_one_edge, slope_two_edge, *sent_edge = call(
@@ -544,14 +588,10 @@
             pieces(2 * MARGIN), pieces(2 * MARGIN),
         ),
         edge_rings,
-        32, 4 * macs, place, top, bottom, kept_one, kept_two, w1, b1, w2, b2,
+        16, 4 * macs, top, bottom, kept_one, kept_two, w1, b1, w2, b2,
     )
     got_edge = [lax.ppermute(sent_edge[k], ("row", "col"), mirror_pairs(k)) for k in range(2)]
 
-    bins = head_weight.shape[0]
-    bins_up = -(-bins // 16) * 16
-    weight = jnp.pad(head_weight, ((0, bins_up - bins), (0, 0)))
-    bias = jnp.pad(head_bias, (0, bins_up - bins), constant_values=-jnp.inf)[:, None]
     delta, first, second = call(
         head_kernel,
         "head",
@@ -560,12 +600,12 @@
             ((width * channels // 2, width), F32), ((size * channels, width), F32),
             ((size, width), jnp.int32),
         ],
-        24, 4 * macs, place, *got_inner, *got_edge, hidden_inner, hidden_edge,
-        slope_two_inner, slope_two_edge, target, weight, weight.T, bias,
+        12, 4 * macs, *got_inner, *got_edge, hidden_inner, hidden_edge,
+        slope_two_inner, slope_two_edge, target, weight, weight_t, bias,
     )
     right, left = shifted(first, "row", -1), shifted(second, "row", 1)
     top, bottom = strips(delta, right, left)
-    w1, w2 = back(first_block_kernel), back(second_block_kernel)
+    w1, w2 = back_1, back_2
     kept_two, kept_one, inner_rows = call(
         backward_inner_kernel,
         "backward_inner",
@@ -574,14 +614,14 @@
             ((size,) + ring, BF16), ((size - 2 * d2,) + ring, BF16),
             ((size + 2 * d2,) + ring, F32),
         ],
-        32, 8 * macs, delta, right, left, slope_one_inner, w2, w1,
+        18, 8 * macs, delta, right, left, slope_one_inner, w2, w1,
     )
     out = call(
         backward_edge_kernel,
         "backward_edge",
         jax.ShapeDtypeStruct((channels * size, width), F32),
         edge_rings,
-        32, 4 * macs, top, bottom, kept_two, kept_one, inner_rows,
+        16, 4 * macs, top, bottom, kept_two, kept_one, inner_rows,
         slope_one_inner, slope_one_edge, w2, w1,
     )
     return out.reshape(channels, size, width)

time: 122 us -> 109 us (0.89)
  local copies, waits for them, and re-layouts: 14.8 us -> 1.25 us
  waiting for transfers between devices: 41.4 us -> 45.2 us
  other arithmetic: 1.63 us -> 0 us
    transpose x7 -> x0, local copies, waits for them, and re-layouts: 5.08 us -> none  [the longest x4 4.82 us: back(): kernel[::-1, ::-1].transpose(0, 3, 1, 2).reshape(3 * channels, 3 * channels)]
    unnamed x26 -> x16, local copies, waits for them, and re-layouts: 6.17 us -> 1.25 us
    ppermute x8, waiting for transfers between devices: 7 us -> 9.54 us  [shifted(): return lax.ppermute(tensor, axis, pairs)]
    reshape x4 -> x0, local copies, waits for them, and re-layouts: 2.51 us -> none  [the longest x2 2.18 us: back(): kernel[::-1, ::-1].transpose(0, 3, 1, 2).reshape(3 * channels, 3 * channels)]
    concatenate x4 -> x0, other arithmetic: 1.55 us -> none  [the longest x2 0.77 us: strips(): jnp.concatenate([main[-MARGIN:], right[-near:], left[-near:]])]
    ppermute x2, waiting for transfers between devices: 26 us -> 27.3 us  [local(): lax.ppermute(sent_inner[k], ('row', 'col'), mirror_pairs(k))]
    pallas_call x6 -> x9, Pallas kernels: 29.1 us -> 27.9 us  [call(): pl.pallas_call(kernel, out_shape=outs, in_specs=[VMEM] * len(operands), o...]
  transfers between devices with their start and end apart: 12 -> 12, of which waited for: 6 -> 9; matrix products, arithmetic and copies ran while one was open for 8% -> 0% of each run, Pallas kernels for 14% -> 15%
where the time goes in v2:
time: 109 us; the launch traced here: 108 us
  waiting for transfers between devices  45.2 us (41%)
  starting transfers between devices  33 us (30%)
  Pallas kernels  27.9 us (26%)
  local copies, waits for them, and re-layouts  1.25 us (1%)
    pallas_call x9, Pallas kernels, call(): pl.pallas_call(kernel, out_shape=outs, in_specs=[VMEM] * len(operands), o...  27.9 us
    ppermute x2, waiting for transfers between devices, local(): lax.ppermute(sent_inner[k], ('row', 'col'), mirror_pairs(k))  27.3 us
    ppermute x8, starting transfers between devices, shifted(): return lax.ppermute(tensor, axis, pairs)  20.5 us
    ppermute x8, waiting for transfers between devices, shifted(): return lax.ppermute(tensor, axis, pairs)  9.54 us
    ppermute x2, waiting for transfers between devices, local(): lax.ppermute(sent_edge[k], ('row', 'col'), mirror_pairs(k))  8.42 us
    ppermute x2, starting transfers between devices, local(): lax.ppermute(sent_edge[k], ('row', 'col'), mirror_pairs(k))  7.89 us
    ppermute x2, starting transfers between devices, local(): lax.ppermute(sent_inner[k], ('row', 'col'), mirror_pairs(k))  4.6 us
  transfers between devices with their start and end apart: 12, of which 9 were waited for; matrix products, arithmetic and copies ran while one was open for 0% of the time, Pallas kernels for 15%

profile of v2, /device:TPU:6, one launch (start us, length us, event | category | flops | bytes accessed | tf_op | source)
XLA Modules:
  0.0 107.6 jit_solution(10261660180324330089)
XLA Ops:
  0.0 1.2 %copy-done = bf16[64,64,128]{2,1,0:T(8,128)(2,1)S(1)} copy-done((bf16[64,64,128]{2,1,0:T(8,128)(2,1)S(1)}, bf16[64,64,128]{2,1,0:T(8,128)(2,1)}, u32[]{:S(2)}) %copy-start) | copy-done | bytes 1048600
  1.3 1.3 %prepare.1 = (bf16[64,64,128]{2,1,0:T(8,128)(2,1)S(1)}, bf16[8,64,128]{2,1,0:T(8,128)(2,1)S(1)}, bf16[8,64,128]{2,1,0:T(8,128)(2,1)S(1)}) custom-call(bf16[64,64,128]{2,1,0:T(8,128)(2,1)S(1)} %copy-done), custom_call_target="tpu_custom_call" | custom-call | flops 1 | bytes 8388608 | tf_op jit(solution)/shard_map/prepare/pallas_call | solution.py:524
  2.5 1.9 %collective-permute-start = (bf16[8,64,128]{2,1,0:T(8,128)(2,1)S(1)}, bf16[8,64,128]{2,1,0:T(8,128)(2,1)S(1)}, u32[]{:S(2)}, u32[]{:S(2)}) collective-permute-start(bf16[8,64,128]{2,1,0:T(8,128)(2,1)S(1)} %get-tuple-element.40), channel_id=1, source_target_pairs={{8,0},{16,8},{24,16},{9,1},{17,9},{25,17},{10,2},{18,10},{26,18},{... | collective-permute-start | bytes 393224 | tf_op jit(solution)/shard_map/ppermute | solution.py:488
  4.5 2.4 %collective-permute-start.1 = (bf16[8,64,128]{2,1,0:T(8,128)(2,1)S(1)}, bf16[8,64,128]{2,1,0:T(8,128)(2,1)S(1)}, u32[]{:S(2)}, u32[]{:S(2)}) collective-permute-start(bf16[8,64,128]{2,1,0:T(8,128)(2,1)S(1)} %get-tuple-element.41), channel_id=1, source_target_pairs={{0,8},{8,16},{16,24},{1,9},{9,17},{17,25},{2,10},{10,18},{18,26},{... | collective-permute-start | bytes 393224 | tf_op jit(solution)/shard_map/ppermute | solution.py:488
  6.9 0.1 collective-permute-done.right_ref
  7.0 3.8 %collective-permute-done.1.left_ref = bf16[8,64,128]{2,1,0:T(8,128)(2,1)S(1)} collective-permute-done((bf16[8,64,128]{2,1,0:T(8,128)(2,1)S(1)}, bf16[8,64,128]{2,1,0:T(8,128)(2,1)S(1)}, u32[]{:S(2)}, u32[]{:S(2)}) %collective-permute-start.1) | collective-permute-done | bytes 131104 | tf_op jit(solution)/shard_map/ppermute | solution.py:488
  10.8 3.5 %collective-permute-start.4 = (bf16[16,64,128]{2,1,0:T(8,128)(2,1)S(1)}, bf16[16,64,128]{2,1,0:T(8,128)(2,1)S(1)}, u32[]{:S(2)}, u32[]{:S(2)}) collective-permute-start(bf16[16,64,128]{2,1,0:T(8,128)(2,1)S(1)} %get-tuple-element.48), channel_id=1, source_target_pairs={{0,1},{1,2},{2,3},{3,4},{4,5},{5,6},{6,7},{8,9},{9,10},{10,11},{11... | collective-permute-start | bytes 786440 | tf_op jit(solution)/shard_map/ppermute | solution.py:488
  14.3 2.4 %collective-permute-start.5 = (bf16[16,64,128]{2,1,0:T(8,128)(2,1)S(1)}, bf16[16,64,128]{2,1,0:T(8,128)(2,1)S(1)}, u32[]{:S(2)}, u32[]{:S(2)}) collective-permute-start(bf16[16,64,128]{2,1,0:T(8,128)(2,1)S(1)} %get-tuple-element.49), channel_id=1, source_target_pairs={{1,0},{2,1},{3,2},{4,3},{5,4},{6,5},{7,6},{9,8},{10,9},{11,10},{12... | collective-permute-start | bytes 786440 | tf_op jit(solution)/shard_map/ppermute | solution.py:488
  16.7 0.4 weights.1
  17.2 7.5 %forward_inner.1 = (f32[2,8,64,256]{3,2,1,0:T(8,128)S(1)}, f32[2,8,64,256]{3,2,1,0:T(8,128)S(1)}, bf16[40,64,128]{2,1,0:T(8,128)(2,1)S(1)}, f32[56,64,256]{2,1,0...) custom-call(bf16[64,64,128]{2,1,0:T(8,128)(2,1)S(1)} %get-tuple-elemen, ...), custom_call_target="tpu_custom_call" | custom-call | flops 2415919104 | bytes 8388608 | tf_op jit(solution)/shard_map/forward_inner/pallas_call | solution.py:524
  24.6 1.9 %collective-permute-start.2 = (bf16[41,32,128]{2,1,0:T(8,128)(2,1)S(1)}, bf16[41,32,128]{2,1,0:T(8,128)(2,1)S(1)}, u32[]{:S(2)}, u32[]{:S(2)}) collective-permute-start(bf16[41,32,128]{2,1,0:T(8,128)(2,1)S(1)} %get-tuple-element.46), channel_id=1, source_target_pairs={{0,0},{8,2},{16,4},{24,6},{1,1},{9,3},{17,5},{25,7},{2,8},{10,10},... | collective-permute-start | bytes 1007624 | tf_op jit(solution)/shard_map/ppermute | solution.py:582
  26.6 2.7 %collective-permute-start.3 = (bf16[41,32,128]{2,1,0:T(8,128)(2,1)S(1)}, bf16[41,32,128]{2,1,0:T(8,128)(2,1)S(1)}, u32[]{:S(2)}, u32[]{:S(2)}) collective-permute-start(bf16[41,32,128]{2,1,0:T(8,128)(2,1)S(1)} %get-tuple-element.47), channel_id=1, source_target_pairs={{0,1},{8,3},{16,5},{24,7},{1,0},{9,2},{17,4},{25,6},{2,9},{10,11},... | collective-permute-start | bytes 1007624 | tf_op jit(solution)/shard_map/ppermute | solution.py:582
  29.2 0.0 collective-permute-done.4.top_ref
  29.3 0.0 collective-permute-done.5.bottom_ref
  29.3 2.3 %forward_edge.1 = (bf16[24,64,128]{2,1,0:T(8,128)(2,1)S(1)}, f32[2,12,64,256]{3,2,1,0:T(8,128)S(1)}, f32[24,64,128]{2,1,0:T(8,128)S(1)}, bf16[24,32,128]{2,1,0:T(8,128)(2,1)S(1)}, bf16[24,32,128]{2,1,0:T(8,128)(2,1)S(1)}) custom-call(bf16[16,64,128]{2,1,0:T(8,128)(2,1)S(1)} %collective-permute-done.4.top_ref, ...), custom_call_target="tpu_custom_call" | custom-call | flops 1207959552 | bytes 8388608 | tf_op jit(solution)/shard_map/forward_edge/pallas_call | solution.py:524
  31.5 3.6 %collective-permute-start.6 = (bf16[24,32,128]{2,1,0:T(8,128)(2,1)S(1)}, bf16[24,32,128]{2,1,0:T(8,128)(2,1)S(1)}, u32[]{:S(2)}, u32[]{:S(2)}) collective-permute-start(bf16[24,32,128]{2,1,0:T(8,128)(2,1)S(1)} %get-tuple-element.52), channel_id=1, source_target_pairs={{0,0},{8,2},{16,4},{24,6},{1,1},{9,3},{17,5},{25,7},{2,8},{10,10},... | collective-permute-start | bytes 589832 | tf_op jit(solution)/shard_map/ppermute | solution.py:593
  35.1 4.3 %collective-permute-start.7 = (bf16[24,32,128]{2,1,0:T(8,128)(2,1)S(1)}, bf16[24,32,128]{2,1,0:T(8,128)(2,1)S(1)}, u32[]{:S(2)}, u32[]{:S(2)}) collective-permute-start(bf16[24,32,128]{2,1,0:T(8,128)(2,1)S(1)} %get-tuple-element.53), channel_id=1, source_target_pairs={{0,1},{8,3},{16,5},{24,7},{1,0},{9,2},{17,4},{25,6},{2,9},{10,11},... | collective-permute-start | bytes 589832 | tf_op jit(solution)/shard_map/ppermute | solution.py:593
  39.4 19.9 %collective-permute-done.2.inner_a_ref = bf16[41,32,128]{2,1,0:T(8,128)(2,1)S(1)} collective-permute-done((bf16[41,32,128]{2,1,0:T(8,128)(2,1)S(1)}, bf16[41,32,128]{2,1,0:T(8,128)(2,1)S(1)}, u32[]{:S(2)}, u32[]{:S(2)}) %collective-permute-start.2) | collective-permute-done | bytes 335904 | tf_op jit(solution)/shard_map/ppermute | solution.py:582
  59.3 7.3 %collective-permute-done.3.inner_b_ref = bf16[41,32,128]{2,1,0:T(8,128)(2,1)S(1)} collective-permute-done((bf16[41,32,128]{2,1,0:T(8,128)(2,1)S(1)}, bf16[41,32,128]{2,1,0:T(8,128)(2,1)S(1)}, u32[]{:S(2)}, u32[]{:S(2)}) %collective-permute-start.3) | collective-permute-done | bytes 335904 | tf_op jit(solution)/shard_map/ppermute | solution.py:582
  66.7 4.1 %collective-permute-done.6.edge_a_ref = bf16[24,32,128]{2,1,0:T(8,128)(2,1)S(1)} collective-permute-done((bf16[24,32,128]{2,1,0:T(8,128)(2,1)S(1)}, bf16[24,32,128]{2,1,0:T(8,128)(2,1)S(1)}, u32[]{:S(2)}, u32[]{:S(2)}) %collective-permute-start.6) | collective-permute-done | bytes 196640 | tf_op jit(solution)/shard_map/ppermute | solution.py:593
  70.8 4.4 %collective-permute-done.7.edge_b_ref = bf16[24,32,128]{2,1,0:T(8,128)(2,1)S(1)} collective-permute-done((bf16[24,32,128]{2,1,0:T(8,128)(2,1)S(1)}, bf16[24,32,128]{2,1,0:T(8,128)(2,1)S(1)}, u32[]{:S(2)}, u32[]{:S(2)}) %collective-permute-start.7) | collective-permute-done | bytes 196640 | tf_op jit(solution)/shard_map/ppermute | solution.py:593
  75.1 6.0 %head.1 = (bf16[64,64,128]{2,1,0:T(8,128)(2,1)S(1)}, bf16[8,64,128]{2,1,0:T(8,128)(2,1)S(1)}, bf16[8,64,128]{2,1,0:T(8,128)(2,1)S(1)}) custom-call(bf16[41,32,128]{2,1,0:T(8,128)(2,1)S(1)} %collective-permute-done.2.inner_a_ref, bf16[41,32,128]{2,1,0:T(8,128)(2,1)S(1)} %collective-permute-done.3.inner_b_ref, ...), custom_call_target="tpu_custom_call" | custom-call | flops 1207959552 | bytes 8388608 | tf_op jit(solution)/shard_map/head/pallas_call | solution.py:524
  81.2 1.9 %collective-permute-start.8 = (bf16[8,64,128]{2,1,0:T(8,128)(2,1)S(1)}, bf16[8,64,128]{2,1,0:T(8,128)(2,1)S(1)}, u32[]{:S(2)}, u32[]{:S(2)}) collective-permute-start(bf16[8,64,128]{2,1,0:T(8,128)(2,1)S(1)} %get-tuple-element.62), channel_id=1, source_target_pairs={{8,0},{16,8},{24,16},{9,1},{17,9},{25,17},{10,2},{18,10},{26,18},{... | collective-permute-start | bytes 393224 | tf_op jit(solution)/shard_map/ppermute | solution.py:488
  83.1 2.4 %collective-permute-start.9 = (bf16[8,64,128]{2,1,0:T(8,128)(2,1)S(1)}, bf16[8,64,128]{2,1,0:T(8,128)(2,1)S(1)}, u32[]{:S(2)}, u32[]{:S(2)}) collective-permute-start(bf16[8,64,128]{2,1,0:T(8,128)(2,1)S(1)} %get-tuple-element.63), channel_id=1, source_target_pairs={{0,8},{8,16},{16,24},{1,9},{9,17},{17,25},{2,10},{10,18},{18,26},{... | collective-permute-start | bytes 393224 | tf_op jit(solution)/shard_map/ppermute | solution.py:488
  85.5 0.1 collective-permute-done.8.right_ref
  85.6 3.8 %collective-permute-done.9.left_ref = bf16[8,64,128]{2,1,0:T(8,128)(2,1)S(1)} collective-permute-done((bf16[8,64,128]{2,1,0:T(8,128)(2,1)S(1)}, bf16[8,64,128]{2,1,0:T(8,128)(2,1)S(1)}, u32[]{:S(2)}, u32[]{:S(2)}) %collective-permute-start.9) | collective-permute-done | bytes 131104 | tf_op jit(solution)/shard_map/ppermute | solution.py:488
  89.4 3.1 %collective-permute-start.10 = (bf16[16,64,128]{2,1,0:T(8,128)(2,1)S(1)}, bf16[16,64,128]{2,1,0:T(8,128)(2,1)S(1)}, u32[]{:S(2)}, u32[]{:S(2)}) collective-permute-start(bf16[16,64,128]{2,1,0:T(8,128)(2,1)S(1)} %get-tuple-element.64), channel_id=1, source_target_pairs={{0,1},{1,2},{2,3},{3,4},{4,5},{5,6},{6,7},{8,9},{9,10},{10,11},{11... | collective-permute-start | bytes 786440 | tf_op jit(solution)/shard_map/ppermute | solution.py:488
  92.6 2.9 %collective-permute-start.11 = (bf16[16,64,128]{2,1,0:T(8,128)(2,1)S(1)}, bf16[16,64,128]{2,1,0:T(8,128)(2,1)S(1)}, u32[]{:S(2)}, u32[]{:S(2)}) collective-permute-start(bf16[16,64,128]{2,1,0:T(8,128)(2,1)S(1)} %get-tuple-element.65), channel_id=1, source_target_pairs={{1,0},{2,1},{3,2},{4,3},{5,4},{6,5},{7,6},{9,8},{10,9},{11,10},{12... | collective-permute-start | bytes 786440 | tf_op jit(solution)/shard_map/ppermute | solution.py:488
  95.5 6.0 %backward_inner.1 = (f32[2,16,64,256]{3,2,1,0:T(8,128)S(1)}, f32[2,4,64,256]{3,2,1,0:T(8,128)S(1)}, f32[40,64,128]{2,1,0:T(8,128)S(1)}) custom-call(bf16[64,64,128]{2,1,0:T(8,128)(2,1)S(1)} %get-tuple-element.61.main_ref, bf16[8,64,128]{2,1,0:T(8,128)(2,1)S(1)} %collective-permute-done.8.right_ref, bf16[8,64,128]{2,1,0:T(8,128)(2,1)S(1)} %collective-permute-done.9.left_ref, ...), custom_call_target="tpu_custom_call" | custom-call | flops 2415919104 | bytes 8388608 | tf_op jit(solution)/shard_map/backward_inner/pallas_call | solution.py:524
  101.5 1.8 %collective-permute-done.10.top_ref = bf16[16,64,128]{2,1,0:T(8,128)(2,1)S(1)} collective-permute-done((bf16[16,64,128]{2,1,0:T(8,128)(2,1)S(1)}, bf16[16,64,128]{2,1,0:T(8,128)(2,1)S(1)}, u32[]{:S(2)}, u32[]{:S(2)}) %collective-permute-start.10) | collective-permute-done | bytes 262176 | tf_op jit(solution)/shard_map/ppermute | solution.py:488
  103.3 0.0 collective-permute-done.11.bottom_ref
  103.3 4.3 %backward_edge.1 = f32[4096,128]{1,0:T(8,128)} custom-call(bf16[16,64,128]{2,1,0:T(8,128)(2,1)S(1)} %collective-permute-done.10.top_ref, bf16[16,64,128]{2,1,0:T(8,128)(2,1)S(1)} %collective-permute-done.11.bottom_ref, f32[2,16,64,256]{3,2,1,0:T(8,128)S(1)} %get-tuple-element.69.kept_two_ref, f32[2,4,64,256]{3,2,1,0:T(8,128)S(1)} %get-tuple-element.70.kept_one_ref, ...), custom_call_target="tpu_custom_call" | custom-call | flops 1207959552 | bytes 8388608 | tf_op jit(solution)/shard_map/backward_edge/pallas_call | solution.py:524
  (17 shorter events, 0.1 us)
Async XLA Ops:
  0.0 1.2 %copy-start = (bf16[64,64,128]{2,1,0:T(8,128)(2,1)S(1)}, bf16[64,64,128]{2,1,0:T(8,128)(2,1)}, u32[]{:S(2)}) copy-start(bf16[64,64,128]{2,1,0:T(8,128)(2,1)} %x_ref.1) | copy-start | bytes 3145732
  1.2 15.4 %copy-start.1 = (bf16[3,3,64,64]{3,2,1,0:T(8,128)(2,1)S(1)}, bf16[3,3,64,64]{3,2,1,0:T(8,128)(2,1)}, u32[]{:S(2)}) copy-start(bf16[3,3,64,64]{3,2,1,0:T(8,128)(2,1)} %k1_ref.1) | copy-start | bytes 221188
  1.2 15.4 %copy-start.2 = (bf16[3,3,64,64]{3,2,1,0:T(8,128)(2,1)S(1)}, bf16[3,3,64,64]{3,2,1,0:T(8,128)(2,1)}, u32[]{:S(2)}) copy-start(bf16[3,3,64,64]{3,2,1,0:T(8,128)(2,1)} %k2_ref.1) | copy-start | bytes 221188
  1.2 15.4 %copy-start.3 = (bf16[37,64]{1,0:T(8,128)(2,1)S(1)}, bf16[37,64]{1,0:T(8,128)(2,1)}, u32[]{:S(2)}) copy-start(bf16[37,64]{1,0:T(8,128)(2,1)} %head_ref.1) | copy-start | bytes 14212
  1.2 15.5 %copy-start.4 = (f32[64]{0:T(128)S(1)}, f32[64]{0:T(128)}, u32[]{:S(2)}) copy-start(f32[64]{0:T(128)} %param.10) | copy-start | bytes 772
  1.2 15.5 %copy-start.5 = (f32[64]{0:T(128)S(1)}, f32[64]{0:T(128)}, u32[]{:S(2)}) copy-start(f32[64]{0:T(128)} %param.12) | copy-start | bytes 772
  1.2 15.5 %copy-start.6 = (f32[37]{0:T(128)S(1)}, f32[37]{0:T(128)}, u32[]{:S(2)}) copy-start(f32[37]{0:T(128)} %param.14) | copy-start | bytes 448
  1.3 15.9 %copy-start.7 = (s32[64,128]{1,0:T(8,128)S(1)}, s32[64,128]{1,0:T(8,128)}, u32[]{:S(2)}) copy-start(s32[64,128]{1,0:T(8,128)} %target_ref.3) | copy-start | bytes 98308
  2.5 4.4 %collective-permute-start = (bf16[8,64,128]{2,1,0:T(8,128)(2,1)S(1)}, bf16[8,64,128]{2,1,0:T(8,128)(2,1)S(1)}, u32[]{:S(2)}, u32[]{:S(2)}) collective-permute-start(bf16[8,64,128]{2,1,0:T(8,128)(2,1)S(1)} %get-tuple-element.40), channel_id=1, source_target_pairs={{8,0},{16,8},{24,16},{9,1},{17,9},{25,17},{10,2},{18,10},{26,18},{... | collective-permute-start | bytes 393224 | tf_op jit(solution)/shard_map/ppermute | solution.py:488
  4.5 6.3 %collective-permute-start.1 = (bf16[8,64,128]{2,1,0:T(8,128)(2,1)S(1)}, bf16[8,64,128]{2,1,0:T(8,128)(2,1)S(1)}, u32[]{:S(2)}, u32[]{:S(2)}) collective-permute-start(bf16[8,64,128]{2,1,0:T(8,128)(2,1)S(1)} %get-tuple-element.41), channel_id=1, source_target_pairs={{0,8},{8,16},{16,24},{1,9},{9,17},{17,25},{2,10},{10,18},{18,26},{... | collective-permute-start | bytes 393224 | tf_op jit(solution)/shard_map/ppermute | solution.py:488
  10.8 18.5 %collective-permute-start.4 = (bf16[16,64,128]{2,1,0:T(8,128)(2,1)S(1)}, bf16[16,64,128]{2,1,0:T(8,128)(2,1)S(1)}, u32[]{:S(2)}, u32[]{:S(2)}) collective-permute-start(bf16[16,64,128]{2,1,0:T(8,128)(2,1)S(1)} %get-tuple-element.48), channel_id=1, source_target_pairs={{0,1},{1,2},{2,3},{3,4},{4,5},{5,6},{6,7},{8,9},{9,10},{10,11},{11... | collective-permute-start | bytes 786440 | tf_op jit(solution)/shard_map/ppermute | solution.py:488
  14.3 15.0 %collective-permute-start.5 = (bf16[16,64,128]{2,1,0:T(8,128)(2,1)S(1)}, bf16[16,64,128]{2,1,0:T(8,128)(2,1)S(1)}, u32[]{:S(2)}, u32[]{:S(2)}) collective-permute-start(bf16[16,64,128]{2,1,0:T(8,128)(2,1)S(1)} %get-tuple-element.49), channel_id=1, source_target_pairs={{1,0},{2,1},{3,2},{4,3},{5,4},{6,5},{7,6},{9,8},{10,9},{11,10},{12... | collective-permute-start | bytes 786440 | tf_op jit(solution)/shard_map/ppermute | solution.py:488
  24.6 34.7 %collective-permute-start.2 = (bf16[41,32,128]{2,1,0:T(8,128)(2,1)S(1)}, bf16[41,32,128]{2,1,0:T(8,128)(2,1)S(1)}, u32[]{:S(2)}, u32[]{:S(2)}) collective-permute-start(bf16[41,32,128]{2,1,0:T(8,128)(2,1)S(1)} %get-tuple-element.46), channel_id=1, source_target_pairs={{0,0},{8,2},{16,4},{24,6},{1,1},{9,3},{17,5},{25,7},{2,8},{10,10},... | collective-permute-start | bytes 1007624 | tf_op jit(solution)/shard_map/ppermute | solution.py:582
  26.6 40.1 %collective-permute-start.3 = (bf16[41,32,128]{2,1,0:T(8,128)(2,1)S(1)}, bf16[41,32,128]{2,1,0:T(8,128)(2,1)S(1)}, u32[]{:S(2)}, u32[]{:S(2)}) collective-permute-start(bf16[41,32,128]{2,1,0:T(8,128)(2,1)S(1)} %get-tuple-element.47), channel_id=1, source_target_pairs={{0,1},{8,3},{16,5},{24,7},{1,0},{9,2},{17,4},{25,6},{2,9},{10,11},... | collective-permute-start | bytes 1007624 | tf_op jit(solution)/shard_map/ppermute | solution.py:582
  31.5 39.2 %collective-permute-start.6 = (bf16[24,32,128]{2,1,0:T(8,128)(2,1)S(1)}, bf16[24,32,128]{2,1,0:T(8,128)(2,1)S(1)}, u32[]{:S(2)}, u32[]{:S(2)}) collective-permute-start(bf16[24,32,128]{2,1,0:T(8,128)(2,1)S(1)} %get-tuple-element.52), channel_id=1, source_target_pairs={{0,0},{8,2},{16,4},{24,6},{1,1},{9,3},{17,5},{25,7},{2,8},{10,10},... | collective-permute-start | bytes 589832 | tf_op jit(solution)/shard_map/ppermute | solution.py:593
  35.1 40.0 %collective-permute-start.7 = (bf16[24,32,128]{2,1,0:T(8,128)(2,1)S(1)}, bf16[24,32,128]{2,1,0:T(8,128)(2,1)S(1)}, u32[]{:S(2)}, u32[]{:S(2)}) collective-permute-start(bf16[24,32,128]{2,1,0:T(8,128)(2,1)S(1)} %get-tuple-element.53), channel_id=1, source_target_pairs={{0,1},{8,3},{16,5},{24,7},{1,0},{9,2},{17,4},{25,6},{2,9},{10,11},... | collective-permute-start | bytes 589832 | tf_op jit(solution)/shard_map/ppermute | solution.py:593
  81.2 4.4 %collective-permute-start.8 = (bf16[8,64,128]{2,1,0:T(8,128)(2,1)S(1)}, bf16[8,64,128]{2,1,0:T(8,128)(2,1)S(1)}, u32[]{:S(2)}, u32[]{:S(2)}) collective-permute-start(bf16[8,64,128]{2,1,0:T(8,128)(2,1)S(1)} %get-tuple-element.62), channel_id=1, source_target_pairs={{8,0},{16,8},{24,16},{9,1},{17,9},{25,17},{10,2},{18,10},{26,18},{... | collective-permute-start | bytes 393224 | tf_op jit(solution)/shard_map/ppermute | solution.py:488
  83.1 6.3 %collective-permute-start.9 = (bf16[8,64,128]{2,1,0:T(8,128)(2,1)S(1)}, bf16[8,64,128]{2,1,0:T(8,128)(2,1)S(1)}, u32[]{:S(2)}, u32[]{:S(2)}) collective-permute-start(bf16[8,64,128]{2,1,0:T(8,128)(2,1)S(1)} %get-tuple-element.63), channel_id=1, source_target_pairs={{0,8},{8,16},{16,24},{1,9},{9,17},{17,25},{2,10},{10,18},{18,26},{... | collective-permute-start | bytes 393224 | tf_op jit(solution)/shard_map/ppermute | solution.py:488
  89.4 13.9 %collective-permute-start.10 = (bf16[16,64,128]{2,1,0:T(8,128)(2,1)S(1)}, bf16[16,64,128]{2,1,0:T(8,128)(2,1)S(1)}, u32[]{:S(2)}, u32[]{:S(2)}) collective-permute-start(bf16[16,64,128]{2,1,0:T(8,128)(2,1)S(1)} %get-tuple-element.64), channel_id=1, source_target_pairs={{0,1},{1,2},{2,3},{3,4},{4,5},{5,6},{6,7},{8,9},{9,10},{10,11},{11... | collective-permute-start | bytes 786440 | tf_op jit(solution)/shard_map/ppermute | solution.py:488
  92.6 10.7 %collective-permute-start.11 = (bf16[16,64,128]{2,1,0:T(8,128)(2,1)S(1)}, bf16[16,64,128]{2,1,0:T(8,128)(2,1)S(1)}, u32[]{:S(2)}, u32[]{:S(2)}) collective-permute-start(bf16[16,64,128]{2,1,0:T(8,128)(2,1)S(1)} %get-tuple-element.65), channel_id=1, source_target_pairs={{1,0},{2,1},{3,2},{4,3},{5,4},{6,5},{7,6},{9,8},{10,9},{11,10},{12... | collective-permute-start | bytes 786440 | tf_op jit(solution)/shard_map/ppermute | solution.py:488

commit v3 on v2

--- a/solution.py
+++ b/solution.py
@@ -488,14 +488,21 @@
     return lax.ppermute(tensor, axis, pairs)
 
 
-def mirror_pairs(step):
+def routes(step):
     col_count, row_count = lax.axis_size("col"), lax.axis_size("row")
     group = col_count // row_count
-    return [
-        (r * col_count + c, (c // group) * col_count + group * r + (c % group + step) % group)
-        for c in range(col_count)
-        for r in range(row_count)
-    ]
+    found = []
+    for c in range(col_count):
+        for r in range(row_count):
+            owner = (c // group) * col_count + group * r + (c % group + step) % group
+            relay = (r + row_count // 2) % row_count * col_count + c
+            found.append((r * col_count + c, relay, owner))
+    return found
+
+
+def hop(tensor, step, begin, end):
+    pairs = [(route[begin], route[end]) for route in routes(step)]
+    return lax.ppermute(tensor, ("row", "col"), pairs)
 
 
 def local(
@@ -540,9 +547,28 @@
 
     packs = rows(size // per)
     square = jax.ShapeDtypeStruct((3 * channels, 3 * channels), BF16)
+    def strips(main, right, left):
+        strip = rows(MARGIN + 2 * -(-MARGIN // per))
+        down, up = call(strips_kernel, "strips", (strip, strip), [], 4, 1, main, right, left)
+        return down, up
+
+    main, first, second = call(
+        prepare_kernel, "prepare", (rows(size), packs, packs), [], 8, 1, pair_features
+    )
+    right, left = shifted(first, "row", -1), shifted(second, "row", 1)
+    down, up = strips(main, right, left)
     bins = head_weight.shape[0]
     bins_up = -(-bins // 16) * 16
     column = jax.ShapeDtypeStruct((channels, width), F32)
+    tensors, down, up = lax.optimization_barrier(
+        (
+            (
+                first_block_kernel, second_block_kernel, first_block_bias[None],
+                second_block_bias[None], head_weight, head_bias[None],
+            ),
+            down, up,
+        )
+    )
     w1, w2, back_1, back_2, b1, b2, weight, weight_t, bias = call(
         weights_kernel,
         "weights",
@@ -552,20 +578,9 @@
             jax.ShapeDtypeStruct((bins_up, width), F32),
         ),
         [((bins_up, channels), F32)],
-        4, macs // 4, first_block_kernel, second_block_kernel, first_block_bias[None],
-        second_block_bias[None], head_weight, head_bias[None],
-    )
-
-    def strips(main, right, left):
-        strip = rows(MARGIN + 2 * -(-MARGIN // per))
-        down, up = call(strips_kernel, "strips", (strip, strip), [], 4, 1, main, right, left)
-        return shifted(down, "col", 1), shifted(up, "col", -1)
-
-    main, first, second = call(
-        prepare_kernel, "prepare", (rows(size), packs, packs), [], 8, 1, pair_features
-    )
-    right, left = shifted(first, "row", -1), shifted(second, "row", 1)
-    top, bottom = strips(main, right, left)
+        4, macs // 4, *tensors,
+    )
+    top, bottom = shifted(down, "col", 1), shifted(up, "col", -1)
     kept_one, kept_two, hidden_inner, slope_one_inner, slope_two_inner, *sent_inner = call(
         forward_inner_kernel,
         "forward_inner",
@@ -579,7 +594,8 @@
         ],
         18, 8 * macs, main, right, left, target, w1, b1, w2, b2,
     )
-    got_inner = [lax.ppermute(sent_inner[k], ("row", "col"), mirror_pairs(k)) for k in range(2)]
+    relayed = hop(sent_inner[0], 0, 0, 1)
+    got_inner_b = hop(sent_inner[1], 1, 0, 2)
     hidden_edge, slope_one_edge, slope_two_edge, *sent_edge = call(
         forward_edge_kernel,
         "forward_edge",
@@ -590,7 +606,9 @@
         edge_rings,
         16, 4 * macs, top, bottom, kept_one, kept_two, w1, b1, w2, b2,
     )
-    got_edge = [lax.ppermute(sent_edge[k], ("row", "col"), mirror_pairs(k)) for k in range(2)]
+    relayed, *sent_edge = lax.optimization_barrier((relayed, *sent_edge))
+    got_inner = [hop(relayed, 0, 1, 2), got_inner_b]
+    got_edge = [hop(sent_edge[k], k, 0, 2) for k in range(2)]
 
     delta, first, second = call(
         head_kernel,
@@ -604,7 +622,8 @@
         slope_two_inner, slope_two_edge, target, weight, weight_t, bias,
     )
     right, left = shifted(first, "row", -1), shifted(second, "row", 1)
-    top, bottom = strips(delta, right, left)
+    down, up = strips(delta, right, left)
+    top, bottom = shifted(down, "col", 1), shifted(up, "col", -1)
     w1, w2 = back_1, back_2
     kept_two, kept_one, inner_rows = call(
         backward_inner_kernel,

time: 109 us -> 94.3 us (0.87)
  waiting for transfers between devices: 45.2 us -> 27.3 us
  starting transfers between devices: 33 us -> 37.3 us
    ppermute x4 -> x5, waiting for transfers between devices: 35.7 us -> 17.7 us  [hop(): return lax.ppermute(tensor, ('row', 'col'), pairs)]
    ppermute x4 -> x5, starting transfers between devices: 12.5 us -> 16.8 us  [hop(): return lax.ppermute(tensor, ('row', 'col'), pairs)]
  transfers between devices with their start and end apart: 12 -> 13, of which waited for: 9 -> 8; matrix products, arithmetic and copies ran while one was open for 0% -> 0% of each run, Pallas kernels for 15% -> 17%
where the time goes in v3:
time: 94.3 us; the launch traced here: 93.9 us
  starting transfers between devices  37.3 us (40%)
  Pallas kernels  27.9 us (30%)
  waiting for transfers between devices  27.3 us (29%)
  local copies, waits for them, and re-layouts  1.25 us (1%)
    pallas_call x9, Pallas kernels, call(): pl.pallas_call(kernel, out_shape=outs, in_specs=[VMEM] * len(operands), o...  27.9 us
    ppermute x8, starting transfers between devices, shifted(): return lax.ppermute(tensor, axis, pairs)  20.5 us
    ppermute x5, waiting for transfers between devices, hop(): return lax.ppermute(tensor, ('row', 'col'), pairs)  17.7 us
    ppermute x5, starting transfers between devices, hop(): return lax.ppermute(tensor, ('row', 'col'), pairs)  16.8 us
    ppermute x8, waiting for transfers between devices, shifted(): return lax.ppermute(tensor, axis, pairs)  9.56 us
  transfers between devices with their start and end apart: 13, of which 8 were waited for; matrix products, arithmetic and copies ran while one was open for 0% of the time, Pallas kernels for 17%

profile of v3, /device:TPU:6, one launch (start us, length us, event | category | flops | bytes accessed | tf_op | source)
XLA Modules:
  0.0 93.9 jit_solution(5193737796560910108)
XLA Ops:
  0.0 1.2 %copy-done = bf16[64,64,128]{2,1,0:T(8,128)(2,1)S(1)} copy-done((bf16[64,64,128]{2,1,0:T(8,128)(2,1)S(1)}, bf16[64,64,128]{2,1,0:T(8,128)(2,1)}, u32[]{:S(2)}) %copy-start) | copy-done | bytes 1048600
  1.3 1.3 %prepare.1 = (bf16[64,64,128]{2,1,0:T(8,128)(2,1)S(1)}, bf16[8,64,128]{2,1,0:T(8,128)(2,1)S(1)}, bf16[8,64,128]{2,1,0:T(8,128)(2,1)S(1)}) custom-call(bf16[64,64,128]{2,1,0:T(8,128)(2,1)S(1)} %copy-done), custom_call_target="tpu_custom_call" | custom-call | flops 1 | bytes 8388608 | tf_op jit(solution)/shard_map/prepare/pallas_call | solution.py:531
  2.5 1.9 %collective-permute-start = (bf16[8,64,128]{2,1,0:T(8,128)(2,1)S(1)}, bf16[8,64,128]{2,1,0:T(8,128)(2,1)S(1)}, u32[]{:S(2)}, u32[]{:S(2)}) collective-permute-start(bf16[8,64,128]{2,1,0:T(8,128)(2,1)S(1)} %get-tuple-element.51), channel_id=1, source_target_pairs={{8,0},{16,8},{24,16},{9,1},{17,9},{25,17},{10,2},{18,10},{26,18},{... | collective-permute-start | bytes 393224 | tf_op jit(solution)/shard_map/ppermute | solution.py:488
  4.5 2.4 %collective-permute-start.1 = (bf16[8,64,128]{2,1,0:T(8,128)(2,1)S(1)}, bf16[8,64,128]{2,1,0:T(8,128)(2,1)S(1)}, u32[]{:S(2)}, u32[]{:S(2)}) collective-permute-start(bf16[8,64,128]{2,1,0:T(8,128)(2,1)S(1)} %get-tuple-element.52), channel_id=1, source_target_pairs={{0,8},{8,16},{16,24},{1,9},{9,17},{17,25},{2,10},{10,18},{18,26},{... | collective-permute-start | bytes 393224 | tf_op jit(solution)/shard_map/ppermute | solution.py:488
  6.9 0.1 collective-permute-done.right_ref
  7.0 3.8 %collective-permute-done.1.left_ref = bf16[8,64,128]{2,1,0:T(8,128)(2,1)S(1)} collective-permute-done((bf16[8,64,128]{2,1,0:T(8,128)(2,1)S(1)}, bf16[8,64,128]{2,1,0:T(8,128)(2,1)S(1)}, u32[]{:S(2)}, u32[]{:S(2)}) %collective-permute-start.1) | collective-permute-done | bytes 131104 | tf_op jit(solution)/shard_map/ppermute | solution.py:488
  10.8 3.5 %collective-permute-start.3 = (bf16[16,64,128]{2,1,0:T(8,128)(2,1)S(1)}, bf16[16,64,128]{2,1,0:T(8,128)(2,1)S(1)}, u32[]{:S(2)}, u32[]{:S(2)}) collective-permute-start(bf16[16,64,128]{2,1,0:T(8,128)(2,1)S(1)} %get-tuple-element.66), channel_id=1, source_target_pairs={{0,1},{1,2},{2,3},{3,4},{4,5},{5,6},{6,7},{8,9},{9,10},{10,11},{11... | collective-permute-start | bytes 786440 | tf_op jit(solution)/shard_map/ppermute | solution.py:488
  14.3 2.4 %collective-permute-start.4 = (bf16[16,64,128]{2,1,0:T(8,128)(2,1)S(1)}, bf16[16,64,128]{2,1,0:T(8,128)(2,1)S(1)}, u32[]{:S(2)}, u32[]{:S(2)}) collective-permute-start(bf16[16,64,128]{2,1,0:T(8,128)(2,1)S(1)} %get-tuple-element.67), channel_id=1, source_target_pairs={{1,0},{2,1},{3,2},{4,3},{5,4},{6,5},{7,6},{9,8},{10,9},{11,10},{12... | collective-permute-start | bytes 786440 | tf_op jit(solution)/shard_map/ppermute | solution.py:488
  16.7 0.4 weights.1
  17.2 7.5 %forward_inner.1 = (f32[2,8,64,256]{3,2,1,0:T(8,128)S(1)}, f32[2,8,64,256]{3,2,1,0:T(8,128)S(1)}, bf16[40,64,128]{2,1,0:T(8,128)(2,1)S(1)}, f32[56,64,256]{2,1,0...) custom-call(bf16[64,64,128]{2,1,0:T(8,128)(2,1)S(1)} %get-tuple-elemen, ...), custom_call_target="tpu_custom_call" | custom-call | flops 2415919104 | bytes 8388608 | tf_op jit(solution)/shard_map/forward_inner/pallas_call | solution.py:531
  24.6 0.1 collective-permute-start.2
  24.7 4.9 %collective-permute-start.6 = (bf16[41,32,128]{2,1,0:T(8,128)(2,1)S(1)}, bf16[41,32,128]{2,1,0:T(8,128)(2,1)S(1)}, u32[]{:S(2)}, u32[]{:S(2)}) collective-permute-start(bf16[41,32,128]{2,1,0:T(8,128)(2,1)S(1)} %get-tuple-element.73), channel_id=1, source_target_pairs={{0,1},{8,3},{16,5},{24,7},{1,0},{9,2},{17,4},{25,6},{2,9},{10,11},... | collective-permute-start | bytes 1007624 | tf_op jit(solution)/shard_map/ppermute | solution.py:505
  29.6 0.0 collective-permute-done.3.top_ref
  29.6 0.0 collective-permute-done.4.bottom_ref
  29.6 2.3 %forward_edge.1 = (bf16[24,64,128]{2,1,0:T(8,128)(2,1)S(1)}, f32[2,12,64,256]{3,2,1,0:T(8,128)S(1)}, f32[24,64,128]{2,1,0:T(8,128)S(1)}, bf16[24,32,128]{2,1,0:T(8,128)(2,1)S(1)}, bf16[24,32,128]{2,1,0:T(8,128)(2,1)S(1)}) custom-call(bf16[16,64,128]{2,1,0:T(8,128)(2,1)S(1)} %collective-permute-done.3.top_ref, ...), custom_call_target="tpu_custom_call" | custom-call | flops 1207959552 | bytes 8388608 | tf_op jit(solution)/shard_map/forward_edge/pallas_call | solution.py:531
  31.9 0.0 collective-permute-done.2
  31.9 1.7 %collective-permute-start.5 = (bf16[41,32,128]{2,1,0:T(8,128)(2,1)S(1)}, bf16[41,32,128]{2,1,0:T(8,128)(2,1)S(1)}, u32[]{:S(2)}, u32[]{:S(2)}) collective-permute-start(bf16[41,32,128]{2,1,0:T(8,128)(2,1)S(1)} %collective-permute-done.2), channel_id=1, source_target_pairs={{16,0},{24,2},{0,4},{8,6},{17,1},{25,3},{1,5},{9,7},{18,8},{26,10}... | collective-permute-start | bytes 1007624 | tf_op jit(solution)/shard_map/ppermute | solution.py:505
  33.6 8.9 %collective-permute-start.7 = (bf16[24,32,128]{2,1,0:T(8,128)(2,1)S(1)}, bf16[24,32,128]{2,1,0:T(8,128)(2,1)S(1)}, u32[]{:S(2)}, u32[]{:S(2)}) collective-permute-start(bf16[24,32,128]{2,1,0:T(8,128)(2,1)S(1)} %get-tuple-element.74), channel_id=1, source_target_pairs={{0,0},{8,2},{16,4},{24,6},{1,1},{9,3},{17,5},{25,7},{2,8},{10,10},... | collective-permute-start | bytes 589832 | tf_op jit(solution)/shard_map/ppermute | solution.py:505
  42.5 1.2 %collective-permute-start.8 = (bf16[24,32,128]{2,1,0:T(8,128)(2,1)S(1)}, bf16[24,32,128]{2,1,0:T(8,128)(2,1)S(1)}, u32[]{:S(2)}, u32[]{:S(2)}) collective-permute-start(bf16[24,32,128]{2,1,0:T(8,128)(2,1)S(1)} %get-tuple-element.75), channel_id=1, source_target_pairs={{0,1},{8,3},{16,5},{24,7},{1,0},{9,2},{17,4},{25,6},{2,9},{10,11},... | collective-permute-start | bytes 589832 | tf_op jit(solution)/shard_map/ppermute | solution.py:505
  43.7 9.5 %collective-permute-done.6.inner_b_ref = bf16[41,32,128]{2,1,0:T(8,128)(2,1)S(1)} collective-permute-done((bf16[41,32,128]{2,1,0:T(8,128)(2,1)S(1)}, bf16[41,32,128]{2,1,0:T(8,128)(2,1)S(1)}, u32[]{:S(2)}, u32[]{:S(2)}) %collective-permute-start.6) | collective-permute-done | bytes 335904 | tf_op jit(solution)/shard_map/ppermute | solution.py:505
  53.2 3.8 %collective-permute-done.7.edge_a_ref = bf16[24,32,128]{2,1,0:T(8,128)(2,1)S(1)} collective-permute-done((bf16[24,32,128]{2,1,0:T(8,128)(2,1)S(1)}, bf16[24,32,128]{2,1,0:T(8,128)(2,1)S(1)}, u32[]{:S(2)}, u32[]{:S(2)}) %collective-permute-start.7) | collective-permute-done | bytes 196640 | tf_op jit(solution)/shard_map/ppermute | solution.py:505
  57.0 4.4 %collective-permute-done.8.edge_b_ref = bf16[24,32,128]{2,1,0:T(8,128)(2,1)S(1)} collective-permute-done((bf16[24,32,128]{2,1,0:T(8,128)(2,1)S(1)}, bf16[24,32,128]{2,1,0:T(8,128)(2,1)S(1)}, u32[]{:S(2)}, u32[]{:S(2)}) %collective-permute-start.8) | collective-permute-done | bytes 196640 | tf_op jit(solution)/shard_map/ppermute | solution.py:505
  61.4 6.0 %head.1 = (bf16[64,64,128]{2,1,0:T(8,128)(2,1)S(1)}, bf16[8,64,128]{2,1,0:T(8,128)(2,1)S(1)}, bf16[8,64,128]{2,1,0:T(8,128)(2,1)S(1)}) custom-call(bf16[41,32,128]{2,1,0:T(8,128)(2,1)S(1)} %collective-permute-done.5.inner_a_ref, bf16[41,32,128]{2,1,0:T(8,128)(2,1)S(1)} %collective-permute-done.6.inner_b_ref, ...), custom_call_target="tpu_custom_call" | custom-call | flops 1207959552 | bytes 8388608 | tf_op jit(solution)/shard_map/head/pallas_call | solution.py:531
  67.5 1.9 %collective-permute-start.9 = (bf16[8,64,128]{2,1,0:T(8,128)(2,1)S(1)}, bf16[8,64,128]{2,1,0:T(8,128)(2,1)S(1)}, u32[]{:S(2)}, u32[]{:S(2)}) collective-permute-start(bf16[8,64,128]{2,1,0:T(8,128)(2,1)S(1)} %get-tuple-element.84), channel_id=1, source_target_pairs={{8,0},{16,8},{24,16},{9,1},{17,9},{25,17},{10,2},{18,10},{26,18},{... | collective-permute-start | bytes 393224 | tf_op jit(solution)/shard_map/ppermute | solution.py:488
  69.4 2.4 %collective-permute-start.10 = (bf16[8,64,128]{2,1,0:T(8,128)(2,1)S(1)}, bf16[8,64,128]{2,1,0:T(8,128)(2,1)S(1)}, u32[]{:S(2)}, u32[]{:S(2)}) collective-permute-start(bf16[8,64,128]{2,1,0:T(8,128)(2,1)S(1)} %get-tuple-element.85), channel_id=1, source_target_pairs={{0,8},{8,16},{16,24},{1,9},{9,17},{17,25},{2,10},{10,18},{18,26},{... | collective-permute-start | bytes 393224 | tf_op jit(solution)/shard_map/ppermute | solution.py:488
  71.8 0.1 collective-permute-done.9.right_ref
  71.9 3.8 %collective-permute-done.10.left_ref = bf16[8,64,128]{2,1,0:T(8,128)(2,1)S(1)} collective-permute-done((bf16[8,64,128]{2,1,0:T(8,128)(2,1)S(1)}, bf16[8,64,128]{2,1,0:T(8,128)(2,1)S(1)}, u32[]{:S(2)}, u32[]{:S(2)}) %collective-permute-start.10) | collective-permute-done | bytes 131104 | tf_op jit(solution)/shard_map/ppermute | solution.py:488
  75.7 3.2 %collective-permute-start.11 = (bf16[16,64,128]{2,1,0:T(8,128)(2,1)S(1)}, bf16[16,64,128]{2,1,0:T(8,128)(2,1)S(1)}, u32[]{:S(2)}, u32[]{:S(2)}) collective-permute-start(bf16[16,64,128]{2,1,0:T(8,128)(2,1)S(1)} %get-tuple-element.86), channel_id=1, source_target_pairs={{0,1},{1,2},{2,3},{3,4},{4,5},{5,6},{6,7},{8,9},{9,10},{10,11},{11... | collective-permute-start | bytes 786440 | tf_op jit(solution)/shard_map/ppermute | solution.py:488
  79.0 2.8 %collective-permute-start.12 = (bf16[16,64,128]{2,1,0:T(8,128)(2,1)S(1)}, bf16[16,64,128]{2,1,0:T(8,128)(2,1)S(1)}, u32[]{:S(2)}, u32[]{:S(2)}) collective-permute-start(bf16[16,64,128]{2,1,0:T(8,128)(2,1)S(1)} %get-tuple-element.87), channel_id=1, source_target_pairs={{1,0},{2,1},{3,2},{4,3},{5,4},{6,5},{7,6},{9,8},{10,9},{11,10},{12... | collective-permute-start | bytes 786440 | tf_op jit(solution)/shard_map/ppermute | solution.py:488
  81.8 6.0 %backward_inner.1 = (f32[2,16,64,256]{3,2,1,0:T(8,128)S(1)}, f32[2,4,64,256]{3,2,1,0:T(8,128)S(1)}, f32[40,64,128]{2,1,0:T(8,128)S(1)}) custom-call(bf16[64,64,128]{2,1,0:T(8,128)(2,1)S(1)} %get-tuple-element.83.main_ref, bf16[8,64,128]{2,1,0:T(8,128)(2,1)S(1)} %collective-permute-done.9.right_ref, bf16[8,64,128]{2,1,0:T(8,128)(2,1)S(1)} %collective-permute-done.10.left_ref, ...), custom_call_target="tpu_custom_call" | custom-call | flops 2415919104 | bytes 8388608 | tf_op jit(solution)/shard_map/backward_inner/pallas_call | solution.py:531
  87.8 1.8 %collective-permute-done.11.top_ref = bf16[16,64,128]{2,1,0:T(8,128)(2,1)S(1)} collective-permute-done((bf16[16,64,128]{2,1,0:T(8,128)(2,1)S(1)}, bf16[16,64,128]{2,1,0:T(8,128)(2,1)S(1)}, u32[]{:S(2)}, u32[]{:S(2)}) %collective-permute-start.11) | collective-permute-done | bytes 262176 | tf_op jit(solution)/shard_map/ppermute | solution.py:488
  89.6 4.3 %backward_edge.1 = f32[4096,128]{1,0:T(8,128)} custom-call(bf16[16,64,128]{2,1,0:T(8,128)(2,1)S(1)} %collective-permute-done.11.top_ref, bf16[16,64,128]{2,1,0:T(8,128)(2,1)S(1)} %collective-permute-done.12.bottom_ref, f32[2,16,64,256]{3,2,1,0:T(8,128)S(1)} %get-tuple-element.91.kept_two_ref, f32[2,4,64,256]{3,2,1,0:T(8,128)S(1)} %get-tuple-element.92.kept_one_ref, ...), custom_call_target="tpu_custom_call" | custom-call | flops 1207959552 | bytes 8388608 | tf_op jit(solution)/shard_map/backward_edge/pallas_call | solution.py:531
  (19 shorter events, 0.1 us)
Async XLA Ops:
  0.0 1.2 %copy-start = (bf16[64,64,128]{2,1,0:T(8,128)(2,1)S(1)}, bf16[64,64,128]{2,1,0:T(8,128)(2,1)}, u32[]{:S(2)}) copy-start(bf16[64,64,128]{2,1,0:T(8,128)(2,1)} %x_ref.1) | copy-start | bytes 3145732
  1.2 15.4 %copy-start.1 = (bf16[3,3,64,64]{3,2,1,0:T(8,128)(2,1)S(1)}, bf16[3,3,64,64]{3,2,1,0:T(8,128)(2,1)}, u32[]{:S(2)}) copy-start(bf16[3,3,64,64]{3,2,1,0:T(8,128)(2,1)} %k1_ref) | copy-start | bytes 221188
  1.2 15.4 %copy-start.2 = (bf16[3,3,64,64]{3,2,1,0:T(8,128)(2,1)S(1)}, bf16[3,3,64,64]{3,2,1,0:T(8,128)(2,1)}, u32[]{:S(2)}) copy-start(bf16[3,3,64,64]{3,2,1,0:T(8,128)(2,1)} %k2_ref) | copy-start | bytes 221188
  1.2 15.4 %copy-start.3 = (bf16[37,64]{1,0:T(8,128)(2,1)S(1)}, bf16[37,64]{1,0:T(8,128)(2,1)}, u32[]{:S(2)}) copy-start(bf16[37,64]{1,0:T(8,128)(2,1)} %head_ref) | copy-start | bytes 14212
  1.2 15.5 %copy-start.4 = (f32[64]{0:T(128)S(1)}, f32[64]{0:T(128)}, u32[]{:S(2)}) copy-start(f32[64]{0:T(128)} %param.10) | copy-start | bytes 772
  1.2 15.5 %copy-start.5 = (f32[64]{0:T(128)S(1)}, f32[64]{0:T(128)}, u32[]{:S(2)}) copy-start(f32[64]{0:T(128)} %param.12) | copy-start | bytes 772
  1.2 15.5 %copy-start.6 = (f32[37]{0:T(128)S(1)}, f32[37]{0:T(128)}, u32[]{:S(2)}) copy-start(f32[37]{0:T(128)} %param.14) | copy-start | bytes 448
  1.3 15.9 %copy-start.7 = (s32[64,128]{1,0:T(8,128)S(1)}, s32[64,128]{1,0:T(8,128)}, u32[]{:S(2)}) copy-start(s32[64,128]{1,0:T(8,128)} %target_ref.3) | copy-start | bytes 98308
  2.5 4.4 %collective-permute-start = (bf16[8,64,128]{2,1,0:T(8,128)(2,1)S(1)}, bf16[8,64,128]{2,1,0:T(8,128)(2,1)S(1)}, u32[]{:S(2)}, u32[]{:S(2)}) collective-permute-start(bf16[8,64,128]{2,1,0:T(8,128)(2,1)S(1)} %get-tuple-element.51), channel_id=1, source_target_pairs={{8,0},{16,8},{24,16},{9,1},{17,9},{25,17},{10,2},{18,10},{26,18},{... | collective-permute-start | bytes 393224 | tf_op jit(solution)/shard_map/ppermute | solution.py:488
  4.5 6.3 %collective-permute-start.1 = (bf16[8,64,128]{2,1,0:T(8,128)(2,1)S(1)}, bf16[8,64,128]{2,1,0:T(8,128)(2,1)S(1)}, u32[]{:S(2)}, u32[]{:S(2)}) collective-permute-start(bf16[8,64,128]{2,1,0:T(8,128)(2,1)S(1)} %get-tuple-element.52), channel_id=1, source_target_pairs={{0,8},{8,16},{16,24},{1,9},{9,17},{17,25},{2,10},{10,18},{18,26},{... | collective-permute-start | bytes 393224 | tf_op jit(solution)/shard_map/ppermute | solution.py:488
  10.8 18.8 %collective-permute-start.3 = (bf16[16,64,128]{2,1,0:T(8,128)(2,1)S(1)}, bf16[16,64,128]{2,1,0:T(8,128)(2,1)S(1)}, u32[]{:S(2)}, u32[]{:S(2)}) collective-permute-start(bf16[16,64,128]{2,1,0:T(8,128)(2,1)S(1)} %get-tuple-element.66), channel_id=1, source_target_pairs={{0,1},{1,2},{2,3},{3,4},{4,5},{5,6},{6,7},{8,9},{9,10},{10,11},{11... | collective-permute-start | bytes 786440 | tf_op jit(solution)/shard_map/ppermute | solution.py:488
  14.3 15.4 %collective-permute-start.4 = (bf16[16,64,128]{2,1,0:T(8,128)(2,1)S(1)}, bf16[16,64,128]{2,1,0:T(8,128)(2,1)S(1)}, u32[]{:S(2)}, u32[]{:S(2)}) collective-permute-start(bf16[16,64,128]{2,1,0:T(8,128)(2,1)S(1)} %get-tuple-element.67), channel_id=1, source_target_pairs={{1,0},{2,1},{3,2},{4,3},{5,4},{6,5},{7,6},{9,8},{10,9},{11,10},{12... | collective-permute-start | bytes 786440 | tf_op jit(solution)/shard_map/ppermute | solution.py:488
  24.6 7.2 %collective-permute-start.2 = (bf16[41,32,128]{2,1,0:T(8,128)(2,1)S(1)}, bf16[41,32,128]{2,1,0:T(8,128)(2,1)S(1)}, u32[]{:S(2)}, u32[]{:S(2)}) collective-permute-start(bf16[41,32,128]{2,1,0:T(8,128)(2,1)S(1)} %get-tuple-element.65), channel_id=1, source_target_pairs={{0,16},{8,24},{16,0},{24,8},{1,17},{9,25},{17,1},{25,9},{2,18},{10... | collective-permute-start | bytes 1007624 | tf_op jit(solution)/shard_map/ppermute | solution.py:505
  24.7 28.5 %collective-permute-start.6 = (bf16[41,32,128]{2,1,0:T(8,128)(2,1)S(1)}, bf16[41,32,128]{2,1,0:T(8,128)(2,1)S(1)}, u32[]{:S(2)}, u32[]{:S(2)}) collective-permute-start(bf16[41,32,128]{2,1,0:T(8,128)(2,1)S(1)} %get-tuple-element.73), channel_id=1, source_target_pairs={{0,1},{8,3},{16,5},{24,7},{1,0},{9,2},{17,4},{25,6},{2,9},{10,11},... | collective-permute-start | bytes 1007624 | tf_op jit(solution)/shard_map/ppermute | solution.py:505
  31.9 29.5 %collective-permute-start.5 = (bf16[41,32,128]{2,1,0:T(8,128)(2,1)S(1)}, bf16[41,32,128]{2,1,0:T(8,128)(2,1)S(1)}, u32[]{:S(2)}, u32[]{:S(2)}) collective-permute-start(bf16[41,32,128]{2,1,0:T(8,128)(2,1)S(1)} %collective-permute-done.2), channel_id=1, source_target_pairs={{16,0},{24,2},{0,4},{8,6},{17,1},{25,3},{1,5},{9,7},{18,8},{26,10}... | collective-permute-start | bytes 1007624 | tf_op jit(solution)/shard_map/ppermute | solution.py:505
  33.6 23.4 %collective-permute-start.7 = (bf16[24,32,128]{2,1,0:T(8,128)(2,1)S(1)}, bf16[24,32,128]{2,1,0:T(8,128)(2,1)S(1)}, u32[]{:S(2)}, u32[]{:S(2)}) collective-permute-start(bf16[24,32,128]{2,1,0:T(8,128)(2,1)S(1)} %get-tuple-element.74), channel_id=1, source_target_pairs={{0,0},{8,2},{16,4},{24,6},{1,1},{9,3},{17,5},{25,7},{2,8},{10,10},... | collective-permute-start | bytes 589832 | tf_op jit(solution)/shard_map/ppermute | solution.py:505
  42.5 18.9 %collective-permute-start.8 = (bf16[24,32,128]{2,1,0:T(8,128)(2,1)S(1)}, bf16[24,32,128]{2,1,0:T(8,128)(2,1)S(1)}, u32[]{:S(2)}, u32[]{:S(2)}) collective-permute-start(bf16[24,32,128]{2,1,0:T(8,128)(2,1)S(1)} %get-tuple-element.75), channel_id=1, source_target_pairs={{0,1},{8,3},{16,5},{24,7},{1,0},{9,2},{17,4},{25,6},{2,9},{10,11},... | collective-permute-start | bytes 589832 | tf_op jit(solution)/shard_map/ppermute | solution.py:505
  67.5 4.4 %collective-permute-start.9 = (bf16[8,64,128]{2,1,0:T(8,128)(2,1)S(1)}, bf16[8,64,128]{2,1,0:T(8,128)(2,1)S(1)}, u32[]{:S(2)}, u32[]{:S(2)}) collective-permute-start(bf16[8,64,128]{2,1,0:T(8,128)(2,1)S(1)} %get-tuple-element.84), channel_id=1, source_target_pairs={{8,0},{16,8},{24,16},{9,1},{17,9},{25,17},{10,2},{18,10},{26,18},{... | collective-permute-start | bytes 393224 | tf_op jit(solution)/shard_map/ppermute | solution.py:488
  69.4 6.3 %collective-permute-start.10 = (bf16[8,64,128]{2,1,0:T(8,128)(2,1)S(1)}, bf16[8,64,128]{2,1,0:T(8,128)(2,1)S(1)}, u32[]{:S(2)}, u32[]{:S(2)}) collective-permute-start(bf16[8,64,128]{2,1,0:T(8,128)(2,1)S(1)} %get-tuple-element.85), channel_id=1, source_target_pairs={{0,8},{8,16},{16,24},{1,9},{9,17},{17,25},{2,10},{10,18},{18,26},{... | collective-permute-start | bytes 393224 | tf_op jit(solution)/shard_map/ppermute | solution.py:488
  75.7 13.9 %collective-permute-start.11 = (bf16[16,64,128]{2,1,0:T(8,128)(2,1)S(1)}, bf16[16,64,128]{2,1,0:T(8,128)(2,1)S(1)}, u32[]{:S(2)}, u32[]{:S(2)}) collective-permute-start(bf16[16,64,128]{2,1,0:T(8,128)(2,1)S(1)} %get-tuple-element.86), channel_id=1, source_target_pairs={{0,1},{1,2},{2,3},{3,4},{4,5},{5,6},{6,7},{8,9},{9,10},{10,11},{11... | collective-permute-start | bytes 786440 | tf_op jit(solution)/shard_map/ppermute | solution.py:488
  79.0 10.6 %collective-permute-start.12 = (bf16[16,64,128]{2,1,0:T(8,128)(2,1)S(1)}, bf16[16,64,128]{2,1,0:T(8,128)(2,1)S(1)}, u32[]{:S(2)}, u32[]{:S(2)}) collective-permute-start(bf16[16,64,128]{2,1,0:T(8,128)(2,1)S(1)} %get-tuple-element.87), channel_id=1, source_target_pairs={{1,0},{2,1},{3,2},{4,3},{5,4},{6,5},{7,6},{9,8},{10,9},{11,10},{12... | collective-permute-start | bytes 786440 | tf_op jit(solution)/shard_map/ppermute | solution.py:488
